TPU v7x, 32 devices: a whole 2x2x4 slice. The times are simulated.
32 devices in a mesh: tm: 8 (over z, core), space: 4 (over y, x).
Axes of the slice: x: 2, y: 2, z: 4, core: 2. Of those that a mesh axis runs over, the one named last changes fastest.
Arguments:
- initial: float32 [2, 128, 512], P(None, 'space'), may hold values from 0.2 to 1
- guess: float32 [128, 2, 128, 512], P('tm', None, 'space'), may hold values from 0 to 1
- kappa: float32 [2, 128, 512], P(None, 'space'), may hold values from 0.005 to 0.05
- feed: float32 [128, 512], P('space'), may hold values from 0.002 to 0.01
- kill: float32 [128, 512], P('space'), may hold values from 0.002 to 0.008
- react: float32 [128, 512], P('space'), may hold values from 0.002 to 0.008
Outputs:
- solution: float32 [128, 2, 128, 512], P('tm', None, 'space')
All inputs are finite; a program needn't handle non-finite values.
Results may differ from a plain program's by a relative error of at most 0.00002.
Values sent between devices are 32-bit elements; how exact they have to be, the bound alone decides.
A program may use at most 128 MiB of HBM per device.

v0:
```python
import jax
import jax.numpy as jnp
from jax import lax
from jax.sharding import PartitionSpec as P

SPAN = 8


def padded_2(block, sides, width):
    for axis, dim in sides:
        count = lax.axis_size(axis)
        forward = [(i, i + 1) for i in range(count - 1)]
        backward = [(target, source) for source, target in forward]
        low = lax.ppermute(
            lax.slice_in_dim(block, block.shape[dim] - width, None, axis=dim), axis, forward
        )
        high = lax.ppermute(lax.slice_in_dim(block, 0, width, axis=dim), axis, backward)
        block = jnp.concatenate([low, block, high], axis=dim)
    return block


def shifted(block, axis, distance):
    devices = range(lax.axis_size(axis))
    route = [(i - distance, i) for i in devices if i - distance in devices]
    return lax.ppermute(block, axis, route)


def coarsen(field):
    shape = field.shape
    blocks = field.reshape(shape[:-2] + (shape[-2] // 2, 2, shape[-1] // 2, 2))
    return blocks.mean(axis=(-3, -1))


def refine(field):
    return jnp.repeat(jnp.repeat(field, 2, axis=-2), 2, axis=-1)


def advance(state, row_padded, coeffs):
    spread, supply, removal, coupling = coeffs
    padded = jnp.pad(row_padded, [(0, 0)] * (row_padded.ndim - 1) + [(1, 1)])
    laplace = (
        padded[..., :-2, 1:-1]
        + padded[..., 2:, 1:-1]
        + padded[..., 1:-1, :-2]
        + padded[..., 1:-1, 2:]
        - 4.0 * state
    )
    first_species = state[..., 0, :, :]
    second_species = state[..., 1, :, :]
    coupled = coupling * first_species * second_species * second_species
    next_first = (
        first_species + spread[0] * laplace[..., 0, :, :] - coupled + supply * (1.0 - first_species)
    )
    next_second = (
        second_species
        + spread[1] * laplace[..., 1, :, :]
        + coupled
        - (supply + removal) * second_species
    )
    return jnp.stack([next_first, next_second], axis=-3)


def margin_advance(state, coeffs, inside_mask):
    row_padded = jnp.pad(state, [(0, 0)] * (state.ndim - 2) + [(1, 1), (0, 0)])
    return advance(state, row_padded, coeffs) * inside_mask


def inside_rows(strip_rows, margin):
    global_rows = (
        lax.axis_index("space") * strip_rows
        - margin
        + jnp.arange(strip_rows + 2 * margin, dtype=jnp.int32)
    )
    inside_mask = (global_rows >= 0) & (global_rows < strip_rows * lax.axis_size("space"))
    return inside_mask.astype(jnp.float32)[:, None]


def split_coeffs(packed):
    return (packed[0:2], packed[2], packed[3], packed[4])


def pack_coeffs(coeffs):
    return jnp.concatenate([coeffs[0], coeffs[1][None], coeffs[2][None], coeffs[3][None]])


def local(initial, guess, kappa, feed, kill, react):
    group = SPAN // 2
    time_index = lax.axis_index("tm")
    opening = time_index == 0
    member = time_index % group
    holder = member == group - 1
    level_zero = (kappa, feed, kill, react)
    spread_one = coarsen(kappa)
    supply_one = coarsen(feed)
    removal_one = coarsen(kill)
    coupling_one = coarsen(react)
    level_one = (2.0 * spread_one, 8.0 * supply_one, 8.0 * removal_one, 8.0 * coupling_one)
    level_two = (
        4.0 * coarsen(spread_one),
        64.0 * coarsen(supply_one),
        64.0 * coarsen(removal_one),
        64.0 * coarsen(coupling_one),
    )
    start_one = coarsen(initial)
    start_two = coarsen(start_one)
    strip_rows = initial.shape[-2]
    mid_rows = strip_rows // 2
    margin = SPAN - 1

    def fine_step(state):
        row_padded = padded_2(state, (("space", 2),), 1)
        return advance(state, row_padded, level_zero)

    def fine_relax(series):
        incoming = shifted(series[-1], "tm", 1)
        incoming = jnp.where(opening, initial, incoming)
        current = jnp.stack([incoming, series[SPAN - 1]])
        early = []
        later = []
        widened = padded_2(current, (("space", 2),), margin)
        for position in range(SPAN - 1):
            widened = margin_advance(widened, fine_wide_coeffs, fine_mask)
            early.append(widened[0, :, margin : margin + strip_rows])
            later.append(widened[1, :, margin : margin + strip_rows])
        return (jnp.stack(early + [series[SPAN - 1]] + later + [series[-1]]), incoming)

    def mid_relax(values):
        predicted = values[1]
        for section in range(group):
            incoming = shifted(values[1], "tm", 1)
            incoming = jnp.where(opening, start_one, incoming)
            widened = padded_2(incoming, (("space", 1),), 2)
            first_wide = margin_advance(widened, mid_wide_coeffs, mid_mask) + mid_wide_forcing[0]
            second_wide = (
                margin_advance(first_wide, mid_wide_coeffs, mid_mask) + mid_wide_forcing[1]
            )
            fresh_first = first_wide[:, 2 : 2 + mid_rows]
            predicted = second_wide[:, 2 : 2 + mid_rows]
            fresh_second = predicted if section < group - 1 else values[1]
            values = jnp.where(member == section, jnp.stack([fresh_first, fresh_second]), values)
        return (values, predicted)

    fine_wide = padded_2(pack_coeffs(level_zero), (("space", 1),), margin)
    fine_wide_coeffs = split_coeffs(fine_wide)
    fine_mask = inside_rows(strip_rows, margin)
    mid_mask = inside_rows(mid_rows, 2)
    series, incoming = fine_relax(guess)
    updated = fine_step(jnp.stack([series[SPAN - 2], series[-2]]))
    series = series.at[SPAN - 1].set(updated[0]).at[-1].set(updated[1])
    series, incoming = fine_relax(series)
    ends = jnp.stack([series[SPAN - 1], series[-1]])
    residual = fine_step(jnp.stack([series[SPAN - 2], series[-2]])) - ends
    restricted = coarsen(ends)
    earlier = jnp.stack([coarsen(incoming), restricted[0]])
    row_padded = padded_2(earlier, (("space", 2),), 1)
    forcing_one = coarsen(residual) + restricted - advance(earlier, row_padded, level_one)
    mid_packed = jnp.concatenate(
        [pack_coeffs(level_one), forcing_one.reshape((4,) + forcing_one.shape[-2:])]
    )
    mid_wide = padded_2(mid_packed, (("space", 1),), 2)
    mid_wide_coeffs = split_coeffs(mid_wide)
    mid_wide_forcing = mid_wide[5:9].reshape((2, 2) + mid_wide.shape[-2:])
    middle, predicted = mid_relax(restricted)
    coarse_values = coarsen(middle[1])
    coarse_right = coarsen(predicted - middle[1]) + coarse_values

    def coarse_step(state):
        row_padded = padded_2(state, (("space", 2),), 1)
        return advance(state, row_padded, level_two)

    def coarse_turn(section, carried):
        current, prior = carried
        arriving = shifted(current, "tm", 1)
        arriving_prior = shifted(prior, "tm", 1)
        arriving = jnp.where(opening, start_two, arriving)
        arriving_prior = jnp.where(opening, start_two, arriving_prior)
        stepped = coarse_step(jnp.stack([arriving, arriving_prior]))
        following = stepped[0] + (coarse_right - stepped[1])
        active = time_index == section
        computes = active & holder
        new_current = jnp.where(computes, following, jnp.where(active, arriving, current))
        new_prior = jnp.where(computes, coarse_values, jnp.where(active, arriving_prior, prior))
        return (new_current, new_prior)

    solved, unused = lax.fori_loop(0, lax.axis_size("tm"), coarse_turn, (start_two, start_two))
    correction = solved - coarse_values
    middle = middle.at[1].set(jnp.where(holder, middle[1] + refine(correction), middle[1]))
    middle, predicted = mid_relax(middle)
    change = refine(middle - restricted)
    series = series.at[SPAN - 1].add(change[0]).at[-1].add(change[1])
    series, incoming = fine_relax(series)
    return series


def solution(mesh):
    in_specs = (
        P(None, "space", None),
        P("tm", None, "space", None),
        P(None, "space", None),
        P("space", None),
        P("space", None),
        P("space", None),
    )
    out_specs = P("tm", None, "space", None)
    return jax.shard_map(local, mesh=mesh, in_specs=in_specs, out_specs=out_specs, check_vma=False)
```

profile of v0, /device:TPU:8, one launch (start us, length us, event | category | flops | bytes accessed | tf_op | source)
XLA Modules:
  0.0 501.7 jit_solution(1638429137506780736)
XLA Ops:
  9.4 6.4 %reshape.348 = f32[16,2,256,2]{3,2,1,0:T(8,128)} reshape(f32[32,512]{1,0:T(8,128)} %param.21) | data formatting | bytes 131072 | tf_op jit(solution)/shard_map/reshape | solution.py:30
  15.8 5.5 %reshape.349 = f32[16,2,256,2]{3,2,1,0:T(8,128)} reshape(f32[32,512]{1,0:T(8,128)S(1)} %copy-done.4) | data formatting | bytes 131072 | tf_op jit(solution)/shard_map/reshape | solution.py:30
  21.3 5.5 %reshape.350 = f32[16,2,256,2]{3,2,1,0:T(8,128)} reshape(f32[32,512]{1,0:T(8,128)S(1)} %copy-done.3) | data formatting | bytes 131072 | tf_op jit(solution)/shard_map/reshape | solution.py:30
  26.9 9.8 %reshape.347 = f32[2,16,2,256,2]{4,3,2,1,0:T(8,128)} reshape(f32[2,32,512]{2,1,0:T(8,128)S(1)} %copy-done.1) | data formatting | bytes 262144 | tf_op jit(solution)/shard_map/reshape | solution.py:30
  45.1 4.6 reduce_sum.137
  58.5 4.8 collective-permute-done.6
  67.5 4.8 collective-permute-start.9
  73.7 9.8 %reshape.345 = f32[2,16,2,256,2]{4,3,2,1,0:T(8,128)} reshape(f32[2,32,512]{2,1,0:T(8,128)S(1)} %copy-done.2) | data formatting | bytes 262144 | tf_op jit(solution)/shard_map/reshape | solution.py:30
  88.6 18.1 %reshape.346 = f32[2,2,16,2,256,2]{5,4,3,2,1,0:T(8,128)} reshape(f32[2,2,32,512]{3,2,1,0:T(8,128)S(1)} %pad_maximum_fusion.10) | data formatting | bytes 524288 | tf_op jit(solution)/shard_map/reshape | solution.py:30
  106.7 8.0 %reduce_sum.136 = f32[2,2,16,256]{3,2,1,0:T(8,128)S(1)} reduce(f32[2,2,16,2,256,2]{5,4,3,2,1,0:T(8,128)} %reshape.346, f32[]{:T(128)} %constant.236.clone.1), dimensions={3,5}, to_apply=%region_1.2 | reduce | flops 49152 | bytes 327684 | tf_op jit(solution)/shard_map/reduce_sum | solution.py:31
  127.1 9.8 %stack.376 = f32[1,2,16,2,256,2]{5,4,3,2,1,0:T(8,128)} reshape(f32[1,2,32,512]{3,2,1,0:T(8,128)S(1)} %get-tuple-element.484) | data formatting | bytes 262144 | tf_op jit(solution)/shard_map/stack | solution.py:151
  136.8 9.7 %stack.375 = f32[1,2,16,2,256,2]{5,4,3,2,1,0:T(8,128)} reshape(f32[1,2,32,512]{3,2,1,0:T(8,128)S(1)} %get-tuple-element.485) | data formatting | bytes 262144 | tf_op jit(solution)/shard_map/stack | solution.py:151
  146.5 5.2 %copy.488 = f32[1,2,16,2,256,2]{4,2,5,3,1,0:T(8,128)S(1)} copy(f32[1,2,16,2,256,2]{5,4,3,2,1,0:T(8,128)} %stack.375) | data formatting | bytes 262144 | tf_op jit(solution)/shard_map/stack | solution.py:151
  151.7 5.9 %copy.489 = f32[1,2,16,2,256,2]{4,2,5,3,1,0:T(8,128)} copy(f32[1,2,16,2,256,2]{5,4,3,2,1,0:T(8,128)} %stack.376) | data formatting | bytes 262144 | tf_op jit(solution)/shard_map/stack | solution.py:151
  157.7 9.8 %reshape.351 = f32[2,16,2,256,2]{4,3,2,1,0:T(8,128)} reshape(f32[2,32,512]{2,1,0:T(8,128)S(1)} %broadcast_select_fusion.2) | data formatting | bytes 262144 | tf_op jit(solution)/shard_map/reshape | solution.py:30
  184.4 5.0 collective-permute-done.16
  193.6 4.8 collective-permute-start.17
  204.5 9.8 %stack.372 = f32[2,1,16,2,256,2]{5,4,3,2,0,1:T(8,128)} reshape(f32[2,1,32,512]{3,2,1,0:T(8,128)S(1)} %get-tuple-element.465) | data formatting | bytes 262144 | tf_op jit(solution)/shard_map/stack | solution.py:60
  214.3 5.2 %copy.486 = f32[2,1,16,2,256,2]{4,2,5,3,1,0:T(8,128)S(1)} copy(f32[2,1,16,2,256,2]{5,4,3,2,0,1:T(8,128)} %stack.372) | data formatting | bytes 262144 | tf_op jit(solution)/shard_map/stack | solution.py:60
  219.5 9.8 %stack.373 = f32[2,1,16,2,256,2]{5,4,3,2,0,1:T(8,128)} reshape(f32[2,1,32,512]{3,2,1,0:T(8,128)S(1)} %get-tuple-element.466) | data formatting | bytes 262144 | tf_op jit(solution)/shard_map/stack | solution.py:60
  229.3 5.3 %copy.487 = f32[2,1,16,2,256,2]{4,2,5,3,1,0:T(8,128)S(1)} copy(f32[2,1,16,2,256,2]{5,4,3,2,0,1:T(8,128)} %stack.373) | data formatting | bytes 262144 | tf_op jit(solution)/shard_map/stack | solution.py:60
  295.3 121.4 %while.22 = (s32[]{:T(128)}, f32[2,8,128]{2,1,0:T(8,128)S(1)}, f32[2,8,128]{2,1,0:T(8,128)S(1)}, s32[]{:T(128)}, pred[]{:T(512)}, /*index=5*/pred[]{:T(512)}, f3...) while((s32[]{:T(128)}, f32[2,8,128]{2,1,0:T(8,128)S(1)}, ...), condition=%wide.region_16.17_spmd, body=%wide.region_15.16_spmd.sunk | while | flops 159524 | bytes 422519 | solution.py:185
  318.0 4.8 collective-permute-start.3
  332.5 5.4 %collective-permute-start.3 = (f32[2,2,1,128]{3,2,1,0:T(1,128)S(1)}, f32[2,2,1,128]{3,2,1,0:T(1,128)S(1)}, u32[]{:S(2)}, u32[]{:S(2)}) collective-permute-start(f32[2,2,1,128]{3,2,1,0:T(1,128)S(1)} %get-tuple-element.659), channel_id=1, source_target_pairs={{0,1},{1,2},{2,3},{4,5},{5,6},{6,7},{8,9},{9,10},{10,11},{12,13},{... | collective-permute-start | bytes 6152 | tf_op jit(solution)/shard_map/while/body/eval_jaxpr/ppermute | solution.py:14
  347.7 5.7 %collective-permute-start.3 = (f32[2,2,1,128]{3,2,1,0:T(1,128)S(1)}, f32[2,2,1,128]{3,2,1,0:T(1,128)S(1)}, u32[]{:S(2)}, u32[]{:S(2)}) collective-permute-start(f32[2,2,1,128]{3,2,1,0:T(1,128)S(1)} %get-tuple-element.659), channel_id=1, source_target_pairs={{0,1},{1,2},{2,3},{4,5},{5,6},{6,7},{8,9},{9,10},{10,11},{12,13},{... | collective-permute-start | bytes 6152 | tf_op jit(solution)/shard_map/while/body/eval_jaxpr/ppermute | solution.py:14
  363.1 5.7 %collective-permute-start.3 = (f32[2,2,1,128]{3,2,1,0:T(1,128)S(1)}, f32[2,2,1,128]{3,2,1,0:T(1,128)S(1)}, u32[]{:S(2)}, u32[]{:S(2)}) collective-permute-start(f32[2,2,1,128]{3,2,1,0:T(1,128)S(1)} %get-tuple-element.659), channel_id=1, source_target_pairs={{0,1},{1,2},{2,3},{4,5},{5,6},{6,7},{8,9},{9,10},{10,11},{12,13},{... | collective-permute-start | bytes 6152 | tf_op jit(solution)/shard_map/while/body/eval_jaxpr/ppermute | solution.py:14
  378.6 5.7 %collective-permute-start.3 = (f32[2,2,1,128]{3,2,1,0:T(1,128)S(1)}, f32[2,2,1,128]{3,2,1,0:T(1,128)S(1)}, u32[]{:S(2)}, u32[]{:S(2)}) collective-permute-start(f32[2,2,1,128]{3,2,1,0:T(1,128)S(1)} %get-tuple-element.659), channel_id=1, source_target_pairs={{0,1},{1,2},{2,3},{4,5},{5,6},{6,7},{8,9},{9,10},{10,11},{12,13},{... | collective-permute-start | bytes 6152 | tf_op jit(solution)/shard_map/while/body/eval_jaxpr/ppermute | solution.py:14
  394.1 5.7 %collective-permute-start.3 = (f32[2,2,1,128]{3,2,1,0:T(1,128)S(1)}, f32[2,2,1,128]{3,2,1,0:T(1,128)S(1)}, u32[]{:S(2)}, u32[]{:S(2)}) collective-permute-start(f32[2,2,1,128]{3,2,1,0:T(1,128)S(1)} %get-tuple-element.659), channel_id=1, source_target_pairs={{0,1},{1,2},{2,3},{4,5},{5,6},{6,7},{8,9},{9,10},{10,11},{12,13},{... | collective-permute-start | bytes 6152 | tf_op jit(solution)/shard_map/while/body/eval_jaxpr/ppermute | solution.py:14
  409.5 5.7 %collective-permute-start.3 = (f32[2,2,1,128]{3,2,1,0:T(1,128)S(1)}, f32[2,2,1,128]{3,2,1,0:T(1,128)S(1)}, u32[]{:S(2)}, u32[]{:S(2)}) collective-permute-start(f32[2,2,1,128]{3,2,1,0:T(1,128)S(1)} %get-tuple-element.659), channel_id=1, source_target_pairs={{0,1},{1,2},{2,3},{4,5},{5,6},{6,7},{8,9},{9,10},{10,11},{12,13},{... | collective-permute-start | bytes 6152 | tf_op jit(solution)/shard_map/while/body/eval_jaxpr/ppermute | solution.py:14
  422.3 5.1 %collective-permute-start.33 = (f32[2,2,256]{2,1,0:T(2,128)S(1)}, f32[2,2,256]{2,1,0:T(2,128)S(1)}, u32[]{:S(2)}, u32[]{:S(2)}) collective-permute-start(f32[2,2,256]{2,1,0:T(2,128)S(1)} %get-tuple-element.539), channel_id=1, source_target_pairs={{0,1},{1,2},{2,3},{4,5},{5,6},{6,7},{8,9},{9,10},{10,11},{12,13},{... | collective-permute-start | bytes 12296 | tf_op jit(solution)/shard_map/ppermute | solution.py:14
  428.8 5.3 %collective-permute-done.34 = f32[2,2,256]{2,1,0:T(2,128)S(1)} collective-permute-done((f32[2,2,256]{2,1,0:T(2,128)S(1)}, f32[2,2,256]{2,1,0:T(2,128)S(1)}, u32[]{:S(2)}, u32[]{:S(2)}) %collective-permute-start.34) | collective-permute-done | bytes 4128 | tf_op jit(solution)/shard_map/ppermute | solution.py:17
  439.8 4.8 collective-permute-start.36
  (548 shorter events, 286.4 us)
Async XLA Ops:
  1.0 50.7 %collective-permute-start.4 = (f32[2,32,512]{2,1,0:T(8,128)S(1)}, f32[2,32,512]{2,1,0:T(8,128)S(1)}, u32[]{:S(2)}, u32[]{:S(2)}) collective-permute-start(f32[2,32,512]{2,1,0:T(8,128)S(1)} %get-tuple-element.421), channel_id=1, source_target_pairs={{0,4},{4,8},{8,12},{12,16},{16,20},{20,24},{24,28},{1,5},{5,9},{9,... | collective-permute-start | bytes 393224 | tf_op jit(solution)/shard_map/ppermute | solution.py:25
  3.8 47.7 %collective-permute-start.7 = (f32[5,7,512]{2,1,0:T(8,128)S(1)}, f32[5,7,512]{2,1,0:T(8,128)S(1)}, u32[]{:S(2)}, u32[]{:S(2)}) collective-permute-start(f32[5,7,512]{2,1,0:T(8,128)S(1)} %get-tuple-element.478), channel_id=1, source_target_pairs={{0,1},{1,2},{2,3},{4,5},{5,6},{6,7},{8,9},{9,10},{10,11},{12,13},{... | collective-permute-start | bytes 215048 | tf_op jit(solution)/shard_map/ppermute | solution.py:14
  7.2 44.3 %collective-permute-start.8 = (f32[5,7,512]{2,1,0:T(8,128)S(1)}, f32[5,7,512]{2,1,0:T(8,128)S(1)}, u32[]{:S(2)}, u32[]{:S(2)}) collective-permute-start(f32[5,7,512]{2,1,0:T(8,128)S(1)} %get-tuple-element.479), channel_id=1, source_target_pairs={{1,0},{2,1},{3,2},{5,4},{6,5},{7,6},{9,8},{10,9},{11,10},{13,12},{... | collective-permute-start | bytes 215048 | tf_op jit(solution)/shard_map/ppermute | solution.py:17
  51.8 6.7 %collective-permute-start.5 = (f32[2,2,7,512]{3,1,2,0:T(2,128)S(1)}, f32[2,2,7,512]{3,1,2,0:T(2,128)S(1)}, u32[]{:S(2)}, u32[]{:S(2)}) collective-permute-start(f32[2,2,7,512]{3,1,2,0:T(2,128)S(1)} %copy.466), channel_id=1, source_target_pairs={{0,1},{1,2},{2,3},{4,5},{5,6},{6,7},{8,9},{9,10},{10,11},{12,13},{... | collective-permute-start | bytes 172040 | tf_op jit(solution)/shard_map/ppermute | solution.py:14
  56.4 6.9 %collective-permute-start.6 = (f32[2,2,7,512]{3,1,2,0:T(2,128)S(1)}, f32[2,2,7,512]{3,1,2,0:T(2,128)S(1)}, u32[]{:S(2)}, u32[]{:S(2)}) collective-permute-start(f32[2,2,7,512]{3,1,2,0:T(2,128)S(1)} %copy.467), channel_id=1, source_target_pairs={{1,0},{2,1},{3,2},{5,4},{6,5},{7,6},{9,8},{10,9},{11,10},{13,12},{... | collective-permute-start | bytes 172040 | tf_op jit(solution)/shard_map/ppermute | solution.py:17
  67.5 20.6 %collective-permute-start.9 = (f32[2,2,1,512]{3,1,2,0:T(2,128)S(1)}, f32[2,2,1,512]{3,1,2,0:T(2,128)S(1)}, u32[]{:S(2)}, u32[]{:S(2)}) collective-permute-start(f32[2,2,1,512]{3,1,2,0:T(2,128)S(1)} %copy.470), channel_id=1, source_target_pairs={{0,1},{1,2},{2,3},{4,5},{5,6},{6,7},{8,9},{9,10},{10,11},{12,13},{... | collective-permute-start | bytes 24584 | tf_op jit(solution)/shard_map/ppermute | solution.py:14
  72.3 15.7 %collective-permute-start.10 = (f32[2,2,1,512]{3,1,2,0:T(2,128)S(1)}, f32[2,2,1,512]{3,1,2,0:T(2,128)S(1)}, u32[]{:S(2)}, u32[]{:S(2)}) collective-permute-start(f32[2,2,1,512]{3,1,2,0:T(2,128)S(1)} %copy.472), channel_id=1, source_target_pairs={{1,0},{2,1},{3,2},{5,4},{6,5},{7,6},{9,8},{10,9},{11,10},{13,12},{... | collective-permute-start | bytes 24584 | tf_op jit(solution)/shard_map/ppermute | solution.py:17
  116.7 41.0 %collective-permute-start.14 = (f32[2,32,512]{2,1,0:T(8,128)S(1)}, f32[2,32,512]{2,1,0:T(8,128)S(1)}, u32[]{:S(2)}, u32[]{:S(2)}) collective-permute-start(f32[2,32,512]{2,1,0:T(8,128)S(1)} %bitcast.149), channel_id=1, source_target_pairs={{0,4},{4,8},{8,12},{12,16},{16,20},{20,24},{24,28},{1,5},{5,9},{9,... | collective-permute-start | bytes 393224 | tf_op jit(solution)/shard_map/ppermute | solution.py:25
  120.9 36.7 %collective-permute-start.12 = (f32[2,2,256]{2,1,0:T(2,128)S(1)}, f32[2,2,256]{2,1,0:T(2,128)S(1)}, u32[]{:S(2)}, u32[]{:S(2)}) collective-permute-start(f32[2,2,256]{2,1,0:T(2,128)S(1)} %get-tuple-element.554), channel_id=1, source_target_pairs={{0,1},{1,2},{2,3},{4,5},{5,6},{6,7},{8,9},{9,10},{10,11},{12,13},{... | collective-permute-start | bytes 12296 | tf_op jit(solution)/shard_map/ppermute | solution.py:14
  125.5 32.1 %collective-permute-start.13 = (f32[2,2,256]{2,1,0:T(2,128)S(1)}, f32[2,2,256]{2,1,0:T(2,128)S(1)}, u32[]{:S(2)}, u32[]{:S(2)}) collective-permute-start(f32[2,2,256]{2,1,0:T(2,128)S(1)} %get-tuple-element.555), channel_id=1, source_target_pairs={{1,0},{2,1},{3,2},{5,4},{6,5},{7,6},{9,8},{10,9},{11,10},{13,12},{... | collective-permute-start | bytes 12296 | tf_op jit(solution)/shard_map/ppermute | solution.py:17
  172.1 11.8 %collective-permute-start.19 = (f32[2,2,1,256]{3,2,1,0:T(1,128)S(1)}, f32[2,2,1,256]{3,2,1,0:T(1,128)S(1)}, u32[]{:S(2)}, u32[]{:S(2)}) collective-permute-start(f32[2,2,1,256]{3,2,1,0:T(1,128)S(1)} %get-tuple-element.529), channel_id=1, source_target_pairs={{0,1},{1,2},{2,3},{4,5},{5,6},{6,7},{8,9},{9,10},{10,11},{12,13},{... | collective-permute-start | bytes 12296 | tf_op jit(solution)/shard_map/ppermute | solution.py:14
  176.6 7.3 %collective-permute-start.20 = (f32[2,2,1,256]{3,2,1,0:T(1,128)S(1)}, f32[2,2,1,256]{3,2,1,0:T(1,128)S(1)}, u32[]{:S(2)}, u32[]{:S(2)}) collective-permute-start(f32[2,2,1,256]{3,2,1,0:T(1,128)S(1)} %get-tuple-element.530), channel_id=1, source_target_pairs={{1,0},{2,1},{3,2},{5,4},{6,5},{7,6},{9,8},{10,9},{11,10},{13,12},{... | collective-permute-start | bytes 12296 | tf_op jit(solution)/shard_map/ppermute | solution.py:17
  178.0 6.4 %collective-permute-start.15 = (f32[2,2,7,512]{3,1,2,0:T(2,128)S(1)}, f32[2,2,7,512]{3,1,2,0:T(2,128)S(1)}, u32[]{:S(2)}, u32[]{:S(2)}) collective-permute-start(f32[2,2,7,512]{3,1,2,0:T(2,128)S(1)} %copy.476), channel_id=1, source_target_pairs={{0,1},{1,2},{2,3},{4,5},{5,6},{6,7},{8,9},{9,10},{10,11},{12,13},{... | collective-permute-start | bytes 172040 | tf_op jit(solution)/shard_map/ppermute | solution.py:14
  182.6 6.8 %collective-permute-start.16 = (f32[2,2,7,512]{3,1,2,0:T(2,128)S(1)}, f32[2,2,7,512]{3,1,2,0:T(2,128)S(1)}, u32[]{:S(2)}, u32[]{:S(2)}) collective-permute-start(f32[2,2,7,512]{3,1,2,0:T(2,128)S(1)} %copy.477), channel_id=1, source_target_pairs={{1,0},{2,1},{3,2},{5,4},{6,5},{7,6},{9,8},{10,9},{11,10},{13,12},{... | collective-permute-start | bytes 172040 | tf_op jit(solution)/shard_map/ppermute | solution.py:17
  193.6 6.4 %collective-permute-start.17 = (f32[2,2,1,512]{3,1,2,0:T(2,128)S(1)}, f32[2,2,1,512]{3,1,2,0:T(2,128)S(1)}, u32[]{:S(2)}, u32[]{:S(2)}) collective-permute-start(f32[2,2,1,512]{3,1,2,0:T(2,128)S(1)} %copy.480), channel_id=1, source_target_pairs={{0,1},{1,2},{2,3},{4,5},{5,6},{6,7},{8,9},{9,10},{10,11},{12,13},{... | collective-permute-start | bytes 24584 | tf_op jit(solution)/shard_map/ppermute | solution.py:14
  272.4 7.6 %collective-permute-start.29 = (f32[2,16,256]{2,1,0:T(8,128)}, f32[2,16,256]{2,1,0:T(8,128)}, u32[]{:S(2)}, u32[]{:S(2)}) collective-permute-start(f32[2,16,256]{2,1,0:T(8,128)} %get-tuple-element.527), channel_id=1, source_target_pairs={{0,4},{4,8},{8,12},{12,16},{16,20},{20,24},{24,28},{1,5},{5,9},{9,... | collective-permute-start | bytes 98312 | tf_op jit(solution)/shard_map/ppermute | solution.py:25
  331.2 6.8 %collective-permute-start.2 = (f32[2,2,1,128]{3,2,1,0:T(1,128)S(1)}, f32[2,2,1,128]{3,2,1,0:T(1,128)S(1)}, u32[]{:S(2)}, u32[]{:S(2)}) collective-permute-start(f32[2,2,1,128]{3,2,1,0:T(1,128)S(1)} %get-tuple-element.658), channel_id=1, source_target_pairs={{1,0},{2,1},{3,2},{5,4},{6,5},{7,6},{9,8},{10,9},{11,10},{13,12},{... | collective-permute-start | bytes 6152 | tf_op jit(solution)/shard_map/while/body/eval_jaxpr/ppermute | solution.py:17
  332.5 6.7 %collective-permute-start.3 = (f32[2,2,1,128]{3,2,1,0:T(1,128)S(1)}, f32[2,2,1,128]{3,2,1,0:T(1,128)S(1)}, u32[]{:S(2)}, u32[]{:S(2)}) collective-permute-start(f32[2,2,1,128]{3,2,1,0:T(1,128)S(1)} %get-tuple-element.659), channel_id=1, source_target_pairs={{0,1},{1,2},{2,3},{4,5},{5,6},{6,7},{8,9},{9,10},{10,11},{12,13},{... | collective-permute-start | bytes 6152 | tf_op jit(solution)/shard_map/while/body/eval_jaxpr/ppermute | solution.py:14
  346.4 7.0 %collective-permute-start.2 = (f32[2,2,1,128]{3,2,1,0:T(1,128)S(1)}, f32[2,2,1,128]{3,2,1,0:T(1,128)S(1)}, u32[]{:S(2)}, u32[]{:S(2)}) collective-permute-start(f32[2,2,1,128]{3,2,1,0:T(1,128)S(1)} %get-tuple-element.658), channel_id=1, source_target_pairs={{1,0},{2,1},{3,2},{5,4},{6,5},{7,6},{9,8},{10,9},{11,10},{13,12},{... | collective-permute-start | bytes 6152 | tf_op jit(solution)/shard_map/while/body/eval_jaxpr/ppermute | solution.py:17
  347.7 7.0 %collective-permute-start.3 = (f32[2,2,1,128]{3,2,1,0:T(1,128)S(1)}, f32[2,2,1,128]{3,2,1,0:T(1,128)S(1)}, u32[]{:S(2)}, u32[]{:S(2)}) collective-permute-start(f32[2,2,1,128]{3,2,1,0:T(1,128)S(1)} %get-tuple-element.659), channel_id=1, source_target_pairs={{0,1},{1,2},{2,3},{4,5},{5,6},{6,7},{8,9},{9,10},{10,11},{12,13},{... | collective-permute-start | bytes 6152 | tf_op jit(solution)/shard_map/while/body/eval_jaxpr/ppermute | solution.py:14
  361.9 7.0 %collective-permute-start.2 = (f32[2,2,1,128]{3,2,1,0:T(1,128)S(1)}, f32[2,2,1,128]{3,2,1,0:T(1,128)S(1)}, u32[]{:S(2)}, u32[]{:S(2)}) collective-permute-start(f32[2,2,1,128]{3,2,1,0:T(1,128)S(1)} %get-tuple-element.658), channel_id=1, source_target_pairs={{1,0},{2,1},{3,2},{5,4},{6,5},{7,6},{9,8},{10,9},{11,10},{13,12},{... | collective-permute-start | bytes 6152 | tf_op jit(solution)/shard_map/while/body/eval_jaxpr/ppermute | solution.py:17
  363.1 7.0 %collective-permute-start.3 = (f32[2,2,1,128]{3,2,1,0:T(1,128)S(1)}, f32[2,2,1,128]{3,2,1,0:T(1,128)S(1)}, u32[]{:S(2)}, u32[]{:S(2)}) collective-permute-start(f32[2,2,1,128]{3,2,1,0:T(1,128)S(1)} %get-tuple-element.659), channel_id=1, source_target_pairs={{0,1},{1,2},{2,3},{4,5},{5,6},{6,7},{8,9},{9,10},{10,11},{12,13},{... | collective-permute-start | bytes 6152 | tf_op jit(solution)/shard_map/while/body/eval_jaxpr/ppermute | solution.py:14
  377.3 7.0 %collective-permute-start.2 = (f32[2,2,1,128]{3,2,1,0:T(1,128)S(1)}, f32[2,2,1,128]{3,2,1,0:T(1,128)S(1)}, u32[]{:S(2)}, u32[]{:S(2)}) collective-permute-start(f32[2,2,1,128]{3,2,1,0:T(1,128)S(1)} %get-tuple-element.658), channel_id=1, source_target_pairs={{1,0},{2,1},{3,2},{5,4},{6,5},{7,6},{9,8},{10,9},{11,10},{13,12},{... | collective-permute-start | bytes 6152 | tf_op jit(solution)/shard_map/while/body/eval_jaxpr/ppermute | solution.py:17
  378.6 7.0 %collective-permute-start.3 = (f32[2,2,1,128]{3,2,1,0:T(1,128)S(1)}, f32[2,2,1,128]{3,2,1,0:T(1,128)S(1)}, u32[]{:S(2)}, u32[]{:S(2)}) collective-permute-start(f32[2,2,1,128]{3,2,1,0:T(1,128)S(1)} %get-tuple-element.659), channel_id=1, source_target_pairs={{0,1},{1,2},{2,3},{4,5},{5,6},{6,7},{8,9},{9,10},{10,11},{12,13},{... | collective-permute-start | bytes 6152 | tf_op jit(solution)/shard_map/while/body/eval_jaxpr/ppermute | solution.py:14
  392.8 7.0 %collective-permute-start.2 = (f32[2,2,1,128]{3,2,1,0:T(1,128)S(1)}, f32[2,2,1,128]{3,2,1,0:T(1,128)S(1)}, u32[]{:S(2)}, u32[]{:S(2)}) collective-permute-start(f32[2,2,1,128]{3,2,1,0:T(1,128)S(1)} %get-tuple-element.658), channel_id=1, source_target_pairs={{1,0},{2,1},{3,2},{5,4},{6,5},{7,6},{9,8},{10,9},{11,10},{13,12},{... | collective-permute-start | bytes 6152 | tf_op jit(solution)/shard_map/while/body/eval_jaxpr/ppermute | solution.py:17
  394.1 7.0 %collective-permute-start.3 = (f32[2,2,1,128]{3,2,1,0:T(1,128)S(1)}, f32[2,2,1,128]{3,2,1,0:T(1,128)S(1)}, u32[]{:S(2)}, u32[]{:S(2)}) collective-permute-start(f32[2,2,1,128]{3,2,1,0:T(1,128)S(1)} %get-tuple-element.659), channel_id=1, source_target_pairs={{0,1},{1,2},{2,3},{4,5},{5,6},{6,7},{8,9},{9,10},{10,11},{12,13},{... | collective-permute-start | bytes 6152 | tf_op jit(solution)/shard_map/while/body/eval_jaxpr/ppermute | solution.py:14
  408.2 7.0 %collective-permute-start.2 = (f32[2,2,1,128]{3,2,1,0:T(1,128)S(1)}, f32[2,2,1,128]{3,2,1,0:T(1,128)S(1)}, u32[]{:S(2)}, u32[]{:S(2)}) collective-permute-start(f32[2,2,1,128]{3,2,1,0:T(1,128)S(1)} %get-tuple-element.658), channel_id=1, source_target_pairs={{1,0},{2,1},{3,2},{5,4},{6,5},{7,6},{9,8},{10,9},{11,10},{13,12},{... | collective-permute-start | bytes 6152 | tf_op jit(solution)/shard_map/while/body/eval_jaxpr/ppermute | solution.py:17
  409.5 7.0 %collective-permute-start.3 = (f32[2,2,1,128]{3,2,1,0:T(1,128)S(1)}, f32[2,2,1,128]{3,2,1,0:T(1,128)S(1)}, u32[]{:S(2)}, u32[]{:S(2)}) collective-permute-start(f32[2,2,1,128]{3,2,1,0:T(1,128)S(1)} %get-tuple-element.659), channel_id=1, source_target_pairs={{0,1},{1,2},{2,3},{4,5},{5,6},{6,7},{8,9},{9,10},{10,11},{12,13},{... | collective-permute-start | bytes 6152 | tf_op jit(solution)/shard_map/while/body/eval_jaxpr/ppermute | solution.py:14
  422.3 6.4 %collective-permute-start.33 = (f32[2,2,256]{2,1,0:T(2,128)S(1)}, f32[2,2,256]{2,1,0:T(2,128)S(1)}, u32[]{:S(2)}, u32[]{:S(2)}) collective-permute-start(f32[2,2,256]{2,1,0:T(2,128)S(1)} %get-tuple-element.539), channel_id=1, source_target_pairs={{0,1},{1,2},{2,3},{4,5},{5,6},{6,7},{8,9},{9,10},{10,11},{12,13},{... | collective-permute-start | bytes 12296 | tf_op jit(solution)/shard_map/ppermute | solution.py:14
  427.4 6.7 %collective-permute-start.34 = (f32[2,2,256]{2,1,0:T(2,128)S(1)}, f32[2,2,256]{2,1,0:T(2,128)S(1)}, u32[]{:S(2)}, u32[]{:S(2)}) collective-permute-start(f32[2,2,256]{2,1,0:T(2,128)S(1)} %get-tuple-element.540), channel_id=1, source_target_pairs={{1,0},{2,1},{3,2},{5,4},{6,5},{7,6},{9,8},{10,9},{11,10},{13,12},{... | collective-permute-start | bytes 12296 | tf_op jit(solution)/shard_map/ppermute | solution.py:17
  439.8 6.1 %collective-permute-start.36 = (f32[2,2,256]{2,1,0:T(2,128)S(1)}, f32[2,2,256]{2,1,0:T(2,128)S(1)}, u32[]{:S(2)}, u32[]{:S(2)}) collective-permute-start(f32[2,2,256]{2,1,0:T(2,128)S(1)} %get-tuple-element.537), channel_id=1, source_target_pairs={{0,1},{1,2},{2,3},{4,5},{5,6},{6,7},{8,9},{9,10},{10,11},{12,13},{... | collective-permute-start | bytes 12296 | tf_op jit(solution)/shard_map/ppermute | solution.py:14
  479.4 6.3 %collective-permute-start.44 = (f32[2,32,512]{2,1,0:T(8,128)S(1)}, f32[2,32,512]{2,1,0:T(8,128)S(1)}, u32[]{:S(2)}, u32[]{:S(2)}) collective-permute-start(f32[2,32,512]{2,1,0:T(8,128)S(1)} %bitcast.152), channel_id=1, source_target_pairs={{0,4},{4,8},{8,12},{12,16},{16,20},{20,24},{24,28},{1,5},{5,9},{9,... | collective-permute-start | bytes 393224 | tf_op jit(solution)/shard_map/ppermute | solution.py:25
  (61 other events, 352.6 us)
where the time goes:
time: 511 us; the launch traced here: 502 us
  starting transfers between devices  200 us (39%)
  local copies, waits for them, and re-layouts  146 us (29%)
  waiting for transfers between devices  97.6 us (19%)
  other arithmetic  54.1 us (11%)
    ppermute x24, starting transfers between devices, padded_2(): lax.ppermute(lax.slice_in_dim(block, block.shape[dim] - width, None, axis...  104 us
    reshape x8, local copies, waits for them, and re-layouts, coarsen(): blocks = field.reshape(shape[:-2] + (shape[-2] // 2, 2, shape[-1] // 2, 2))  67 us
    ppermute x27, starting transfers between devices, shifted(): return lax.ppermute(block, axis, route)  63.6 us
    ppermute x24, waiting for transfers between devices, padded_2(): lax.ppermute(lax.slice_in_dim(block, 0, width, axis=dim), axis, backward)  51.2 us
    ppermute x27, waiting for transfers between devices, shifted(): return lax.ppermute(block, axis, route)  35.3 us
    reduce_sum x15, other arithmetic, coarsen(): return blocks.mean(axis=(-3, -1))  32.1 us
    ppermute x24, starting transfers between devices, padded_2(): lax.ppermute(lax.slice_in_dim(block, 0, width, axis=dim), axis, backward)  32.1 us
    another operation x4, local copies, waits for them, and re-layouts, local(): ends = jnp.stack([series[SPAN - 1], series[-1]])  30.6 us
  transfers between devices with their start and end apart: 75, of which 38 were waited for; matrix products, arithmetic and copies ran while one was open for 20% of the time, Pallas kernels for 0%

commit v1 on v0

v1 whole, which is shorter than its diff:
```python
import jax
import jax.numpy as jnp
from jax import lax
from jax.experimental import pallas as pl
from jax.experimental.pallas import tpu as pltpu
from jax.sharding import PartitionSpec as P

SPAN = 8
H = 8
GROUP = SPAN // 2
MESH = pl.DeviceIdType.MESH
F32 = jnp.float32


def phi(src, coef, quad, first, last, total, emit):
    cols = src.shape[-1]
    lane = lax.broadcasted_iota(jnp.int32, (8, cols), 1)
    row = lax.broadcasted_iota(jnp.int32, (8, cols), 0)
    cache = {}

    def load(b, sp):
        b = b % total
        if (b, sp) not in cache:
            x = src[sp, b * 8 : b * 8 + 8, :]
            cache[b, sp] = (x, pltpu.roll(x, 1, 0), pltpu.roll(x, 7, 0))
        return cache[b, sp]

    for blk in range(first, last):
        rows = slice(blk * 8, blk * 8 + 8)
        x = []
        around = []
        for sp in range(2):
            v, down, up = load(blk, sp)
            above = jnp.where(row == 0, load(blk - 1, sp)[1], down)
            below = jnp.where(row == 7, load(blk + 1, sp)[2], up)
            left = jnp.where(lane == 0, 0.0, pltpu.roll(v, 1, 1))
            right = jnp.where(lane == cols - 1, 0.0, pltpu.roll(v, cols - 1, 1))
            x.append(v)
            around.append((above + below) + (left + right))
        c = coef[4, rows, :] * x[0] * (x[1] * x[1])
        emit(blk, 0, quad[0, rows, :] * x[0] + coef[0, rows, :] * around[0] + (coef[2, rows, :] - c))
        emit(blk, 1, quad[1, rows, :] * x[1] + coef[1, rows, :] * around[1] + c)


def into(dst, shift=0):
    def emit(b, sp, value):
        dst[sp, b * 8 + shift : b * 8 + shift + 8, :] = value

    return emit


def pieces(x):
    t = x * 65537.0
    a = t - (t - x)
    r = x - a
    t = r * 65537.0
    b = t - (t - r)
    return [a, b, r - b]


def times(x, matrix):
    n = x.shape[0]
    y = jnp.dot(jnp.concatenate(pieces(x), 0), matrix, preferred_element_type=F32)
    return y[:n] + y[n : 2 * n] + y[2 * n :]


def row_matrix(out_rows, in_rows, shift, expand):
    i = lax.broadcasted_iota(jnp.int32, (out_rows, in_rows), 0)
    j = lax.broadcasted_iota(jnp.int32, (out_rows, in_rows), 1)
    d = (i - 2 * j if expand else j - 2 * i) + shift
    m = jnp.where((d == 0) | (d == 1), 1.0 if expand else 0.25, 0.0)
    return jnp.concatenate([m, m, m], 1)


def rows_times(matrix, x):
    return jnp.dot(matrix, jnp.concatenate(pieces(x), 0), preferred_element_type=F32)


def coarsen(xs, wide, cmat):
    rows, cols = xs[0].shape
    out_rows = (rows - 2 * H) // 2 + 2 * H if wide else rows // 2
    m = row_matrix(out_rows, rows, H if wide else 0, False)
    y = times(jnp.concatenate(xs, 0), cmat[0:cols, 0 : cols // 2])
    return [rows_times(m, y[k * rows : (k + 1) * rows]) for k in range(len(xs))]


def refine(xs, emat):
    rows, cols = xs[0].shape
    out_rows = (rows - 2 * H) * 2 + 2 * H
    m = row_matrix(out_rows, rows, H, True)
    y = jnp.concatenate([rows_times(m, x) for x in xs], 0)
    z = times(y, emat[0:cols, 0 : 2 * cols])
    return [z[k * out_rows : (k + 1) * out_rows] for k in range(len(xs))]


def kernel(
    T, S,
    initial, guess, kappa, feed, kill, react, out,
    cf, q0, c1, q1, c2, q2, ga, gb, ca, cb, cc, dd, st0, st1, outbuf,
    wa, wb, wc, gs, vs, vv, dl, ei, eo, zz, zy, cmat, emat,
    s_loc, s_cf, r_cf, s_g, r_g, s_c1, r_c1, s_ca, r_ca, s_cb, r_cb,
    s_vs, r_vs, s_gs, r_gs, s_e, r_e, s_d, r_d, s_out,
):
    t = lax.axis_index("tm")
    s = lax.axis_index("space")
    m = lax.rem(t, GROUP)
    base = t - m
    N = cf.shape[1] - 2 * H
    N1 = c1.shape[1] - 2 * H
    N2 = ei.shape[1] - 2 * H
    has = {-1: s > 0, 1: s < S - 1, 0: t >= 0}
    opening = t == 0
    sends = []

    def edge(n, ds):
        if ds == -1:
            return slice(0, H), slice(n + H, n + 2 * H)
        if ds == 1:
            return slice(n - H, n), slice(0, H)
        return slice(0, n), slice(H, n + H)

    def shift(sl, by):
        return slice(sl.start + by, sl.stop + by)

    def send(cond, src, dst, ssem, rsem, dt, ds):
        copy = pltpu.make_async_remote_copy(
            src_ref=src, dst_ref=dst, send_sem=ssem, recv_sem=rsem,
            device_id=(t + dt, s + ds), device_id_type=MESH,
        )

        @pl.when(cond)
        def _():
            copy.start()

        sends.append((cond, copy))

    def arrive(cond, dst, rsem):
        @pl.when(cond)
        def _():
            pltpu.make_async_copy(dst, dst, rsem).wait()

    mid = slice(H, N + H)
    local = [
        pltpu.make_async_copy(guess.at[SPAN - 1], gb.at[:, mid], s_loc.at[0]),
        pltpu.make_async_copy(kappa, cf.at[0:2, mid], s_loc.at[1]),
        pltpu.make_async_copy(feed, cf.at[2, mid], s_loc.at[2]),
        pltpu.make_async_copy(kill, cf.at[3, mid], s_loc.at[3]),
        pltpu.make_async_copy(react, cf.at[4, mid], s_loc.at[4]),
    ]
    for c in local:
        c.start()
    opened = [
        pltpu.make_async_copy(initial, ga.at[:, mid], s_loc.at[5]),
        pltpu.make_async_copy(initial, ca.at[:, mid], s_loc.at[6]),
    ]

    @pl.when(opening)
    def _():
        for c in opened:
            c.start()

    for ds in (-1, 1):
        @pl.when(jnp.logical_not(has[ds]))
        def _():
            for ref, n in ((cf, N), (ga, N), (gb, N), (ca, N), (cb, N), (c1, N1), (vs, N1)):
                rows = slice(0, H) if ds == -1 else slice(n + H, n + 2 * H)
                ref[:, rows, :] = jnp.zeros((ref.shape[0], H, ref.shape[2]), F32)
            rows = slice(0, H) if ds == -1 else slice(N1 + H, N1 + 2 * H)
            gs[:, :, rows, :] = jnp.zeros((SPAN, 2, H, gs.shape[3]), F32)
            dl[:, :, rows, :] = jnp.zeros((2, 2, H, dl.shape[3]), F32)
            rows = slice(0, H) if ds == -1 else slice(N2 + H, N2 + 2 * H)
            ei[:, rows, :] = jnp.zeros((2, H, ei.shape[2]), F32)

    @pl.when(base == 0)
    def _():
        ei[...] = jnp.zeros(ei.shape, F32)

    barrier = pltpu.get_barrier_semaphore()
    count = jnp.int32(0)
    for dt in range(-GROUP, GROUP + 1):
        other = t + dt
        known = (other >= 0) & (other < T)
        if abs(dt) not in (0, 1, GROUP):
            known = known & (m + dt >= 0) & (m + dt < GROUP)
        for ds in (-1, 0, 1):
            if dt == 0 and ds == 0:
                continue
            there = known & has[ds]

            @pl.when(there)
            def _():
                pl.semaphore_signal(barrier, inc=1, device_id=(other, s + ds), device_id_type=MESH)

            count = count + there.astype(jnp.int32)
    pl.semaphore_wait(barrier, count)

    further = t < T - 1
    for ds in (-1, 1):
        src, dst = edge(N, ds)
        k = (ds + 1) // 2
        send(has[ds], guess.at[SPAN - 1, :, src], gb.at[:, dst], s_cf.at[k, 4], r_cf.at[k, 4], 0, ds)
        send(has[ds], kappa.at[:, src], cf.at[0:2, dst], s_cf.at[k, 0], r_cf.at[k, 0], 0, ds)
        send(has[ds], feed.at[src], cf.at[2, dst], s_cf.at[k, 1], r_cf.at[k, 1], 0, ds)
        send(has[ds], kill.at[src], cf.at[3, dst], s_cf.at[k, 2], r_cf.at[k, 2], 0, ds)
        send(has[ds], react.at[src], cf.at[4, dst], s_cf.at[k, 3], r_cf.at[k, 3], 0, ds)
    for ds in (0, -1, 1):
        src, dst = edge(N, ds)
        k = ds + 1
        send(further & has[ds], guess.at[2 * SPAN - 1, :, src], ga.at[:, dst], s_g.at[0, k], r_g.at[k], 1, ds)
        if ds:
            send(opening & has[ds], initial.at[:, src], ga.at[:, dst], s_g.at[1, k], r_g.at[k], 0, ds)
            send(opening & has[ds], initial.at[:, src], ca.at[:, dst], s_g.at[2, k], r_ca.at[k], 0, ds)

    ii = lax.broadcasted_iota(jnp.int32, cmat.shape, 0) - 2 * lax.broadcasted_iota(jnp.int32, cmat.shape, 1)
    cmat[...] = jnp.where((ii == 0) | (ii == 1), 1.0, 0.0)
    jj = lax.broadcasted_iota(jnp.int32, emat.shape, 1) - 2 * lax.broadcasted_iota(jnp.int32, emat.shape, 0)
    emat[...] = jnp.where((jj == 0) | (jj == 1), 1.0, 0.0)
    eo[...] = jnp.zeros(eo.shape, F32)

    for c in local:
        c.wait()
    for ds in (-1, 1):
        k = (ds + 1) // 2
        dst = edge(N, ds)[1]
        arrive(has[-ds], gb.at[:, dst], r_cf.at[k, 4])
        arrive(has[-ds], cf.at[0:2, dst], r_cf.at[k, 0])
        arrive(has[-ds], cf.at[2, dst], r_cf.at[k, 1])
        arrive(has[-ds], cf.at[3, dst], r_cf.at[k, 2])
        arrive(has[-ds], cf.at[4, dst], r_cf.at[k, 3])

    def quads(coef, quad):
        quad[0] = 1.0 - coef[2] - 4.0 * coef[0]
        quad[1] = 1.0 - (coef[2] + coef[3]) - 4.0 * coef[1]

    quads(cf, q0)
    blocks = (N + 2 * H) // 8

    def interval(src, emit):
        phi(src, cf, q0, 0, blocks, blocks, into(st0))

        @pl.loop(0, 3)
        def _(_):
            phi(st0, cf, q0, 0, blocks, blocks, into(st1))
            phi(st1, cf, q0, 0, blocks, blocks, into(st0))

        phi(st0, cf, q0, 1, blocks - 1, blocks, emit)

    interval(gb, into(cc, -H))
    for ds in (0, -1, 1):
        src, dst = edge(N, ds)
        send(further & has[ds], cc.at[:, src], ca.at[:, dst], s_ca.at[ds + 1], r_ca.at[ds + 1], 1, ds)

    scale = (2.0, 2.0, 8.0, 8.0, 8.0)
    for k, x in enumerate(coarsen([cf[k, mid, :] for k in range(5)], False, cmat)):
        c1[k, H : H + N1, :] = scale[k] * x
    for ds in (-1, 1):
        src, dst = edge(N1, ds)
        k = (ds + 1) // 2
        send(has[ds], c1.at[:, shift(src, H)], c1.at[:, dst], s_c1.at[k], r_c1.at[k], 0, ds)
    for k, x in enumerate(coarsen([c1[k, H : H + N1, :] for k in range(5)], False, cmat)):
        c2[k, H : H + N2, :] = scale[k] * x
    q2[0, H : H + N2, :] = 1.0 - c2[2, H : H + N2, :] - 4.0 * c2[0, H : H + N2, :]
    q2[1, H : H + N2, :] = 1.0 - (c2[2, H : H + N2, :] + c2[3, H : H + N2, :]) - 4.0 * c2[1, H : H + N2, :]

    for c in opened:
        @pl.when(opening)
        def _():
            c.wait()
    for ds in (-1, 0, 1):
        cond = has[-ds] if ds else jnp.logical_not(opening)
        arrive(cond, ga.at[:, edge(N, ds)[1]], r_g.at[ds + 1])
    interval(ga, into(cb))
    for ds in (-1, 1):
        src, dst = edge(N, ds)
        k = (ds + 1) // 2
        send(has[ds], cb.at[:, shift(src, H)], cb.at[:, dst], s_cb.at[k], r_cb.at[k], 0, ds)
    for k, x in enumerate(coarsen([cc[0], cc[1]], False, cmat)):
        wc[k] = x
    for ds in (-1, 1):
        arrive(has[-ds], c1.at[:, edge(N1, ds)[1]], r_c1.at[(ds + 1) // 2])
    quads(c1, q1)
    blocks1 = (N1 + 2 * H) // 8

    for ds in (-1, 0, 1):
        cond = has[-ds] if ds else jnp.logical_not(opening)
        arrive(cond, ca.at[:, edge(N, ds)[1]], r_ca.at[ds + 1])
    for k, x in enumerate(coarsen([ca[0], ca[1]], True, cmat)):
        wa[k] = x
    first = m == 0

    @pl.when(first)
    def _():
        vs[:, H : H + N1, :] = wa[:, H : H + N1, :]

    for dm in range(GROUP):
        for ds in (0, -1, 1):
            if dm or ds:
                src, dst = edge(N1, ds)
                send(first & has[ds], wa.at[:, shift(src, H)], vs.at[:, dst],
                     s_vs.at[dm, ds + 1], r_vs.at[ds + 1], dm, ds)

    def forcing(which, w, start):
        interval(start, into(dd, -H))
        slot = 2 * m + which
        r = coarsen([dd[0], dd[1]], False, cmat)
        last = jnp.where(m == GROUP - 1, 1.0, 0.0) if which else None

        def emit(b, sp, value):
            rows = slice(b * 8 - H, b * 8 - H + 8)
            g = r[sp][rows] - value
            if which:
                g = g - last * wc[sp, rows, :]
            gs[slot, sp, b * 8 : b * 8 + 8, :] = g

        phi(w, c1, q1, 1, blocks1 - 1, blocks1, emit)
        for dm in range(-GROUP + 1, GROUP):
            inside = (m + dm >= 0) & (m + dm < GROUP)
            for ds in (0, -1, 1):
                if dm or ds:
                    src, dst = edge(N1, ds)
                    send(inside & has[ds], gs.at[slot, :, shift(src, H)], gs.at[slot, :, dst],
                         s_gs.at[which, dm + GROUP - 1, ds + 1], r_gs.at[slot, ds + 1], dm, ds)

    forcing(0, wa, ca)
    for ds in (-1, 1):
        arrive(has[-ds], cb.at[:, edge(N, ds)[1]], r_cb.at[(ds + 1) // 2])
    for k, x in enumerate(coarsen([cb[0], cb[1]], True, cmat)):
        wb[k] = x
    forcing(1, wb, cb)

    for ds in (0, -1, 1):
        cond = has[-ds] if ds else jnp.logical_not(first)
        arrive(cond, vs.at[:, edge(N1, ds)[1]], r_vs.at[ds + 1])
    vv[0] = vs[...]

    def middle_step(i, wait):
        if wait:
            for ds in (0, -1, 1):
                cond = has[-ds] if ds else (m != i // 2)
                arrive(cond, gs.at[i, :, edge(N1, ds)[1]], r_gs.at[i, ds + 1])

        def emit(b, sp, value):
            rows = slice(b * 8, b * 8 + 8)
            vv[i + 1, sp, rows, :] = value + gs[i, sp, rows, :]

        phi(vv.at[i], c1, q1, 0, blocks1, blocks1, emit)

    for i in range(SPAN):
        middle_step(i, True)

    r = coarsen([vv[SPAN, sp, H : H + N1, :] for sp in range(2)], False, cmat)
    z = coarsen([vs[0], vs[1]], True, cmat)
    for ds in (-1, 0, 1):
        cond = (base > 0) & has[-ds]
        arrive(cond, ei.at[:, edge(N2, ds)[1]], r_e.at[ds + 1])
    for sp in range(2):
        zz[sp] = z[sp]
        zy[sp] = z[sp] + ei[sp]
    top = (N2 + 2 * H) // 8

    def emit_old(b, sp, value):
        eo[sp, b * 8 : b * 8 + 8, :] = r[sp][b * 8 - H : b * 8 - H + 8] - value

    def emit_new(b, sp, value):
        rows = slice(b * 8, b * 8 + 8)
        eo[sp, rows, :] = eo[sp, rows, :] + value

    phi(zz, c2, q2, 1, top - 1, top, emit_old)
    phi(zy, c2, q2, 1, top - 1, top, emit_new)
    for ds in (0, -1, 1):
        src, dst = edge(N2, ds)
        send((t + GROUP < T) & has[ds], eo.at[:, shift(src, H)], ei.at[:, dst],
             s_e.at[ds + 1], r_e.at[ds + 1], GROUP, ds)

    p = refine([ei[0], ei[1]], emat)
    for sp in range(2):
        vv[0, sp] = vs[sp] + p[sp]
    for i in range(SPAN - 1):
        middle_step(i, False)
    p = refine([eo[0], eo[1]], emat)
    for sp in range(2):
        vv[SPAN, sp, H : H + N1, :] = wc[sp] + p[sp][H : H + N1]
    inner = slice(H, H + N1)
    dl[0, :, inner, :] = vv[2 * m, :, inner, :] - wa[:, inner, :]
    dl[1, :, inner, :] = vv[2 * m + 1, :, inner, :] - wb[:, inner, :]
    for ds in (-1, 1):
        src, dst = edge(N1, ds)
        k = (ds + 1) // 2
        send(has[ds], dl.at[:, :, shift(src, H)], dl.at[:, :, dst], s_d.at[k], r_d.at[k], 0, ds)

    def done(i):
        return pltpu.make_async_copy(outbuf.at[i], out.at[i], s_out.at[i])

    zeros = jnp.zeros((H, c1.shape[2]), F32)
    tail = [
        jnp.concatenate([zeros, vv[2 * m + 2, sp, inner, :] - wc[sp], zeros], 0) for sp in range(2)
    ]
    p = refine(tail, emat)
    for sp in range(2):
        outbuf[2 * SPAN - 1, sp] = cc[sp] + p[sp][mid]
    done(2 * SPAN - 1).start()

    for ds in (-1, 1):
        arrive(has[-ds], dl.at[:, :, edge(N1, ds)[1]], r_d.at[(ds + 1) // 2])
    p = refine([dl[0, 0], dl[0, 1], dl[1, 0], dl[1, 1]], emat)
    for sp in range(2):
        ga[sp] = ca[sp] + p[sp]
        u = cb[sp] + p[2 + sp]
        gb[sp] = u
        outbuf[SPAN - 1, sp] = u[mid]
    done(SPAN - 1).start()

    def final(src, at):
        def step(a, b, i):
            def emit(blk, sp, value):
                b[sp, blk * 8 : blk * 8 + 8, :] = value
                if 1 <= blk < blocks - 1:
                    outbuf[i, sp, blk * 8 - H : blk * 8 - H + 8, :] = value

            phi(a, cf, q0, 0, blocks, blocks, emit)
            done(i).start()

        step(src, st0, at)

        @pl.loop(0, 3)
        def _(k):
            step(st0, st1, at + 1 + 2 * k)
            step(st1, st0, at + 2 + 2 * k)

    final(ga, 0)
    final(gb, SPAN)
    for i in range(2 * SPAN):
        done(i).wait()
    for cond, copy in sends:
        @pl.when(cond)
        def _():
            copy.wait_send()


def local(T, S, initial, guess, kappa, feed, kill, react):
    _, N, C = initial.shape
    W, W1, W2 = N + 2 * H, N // 2 + 2 * H, N // 4 + 2 * H
    C1, C2 = C // 2, C // 4
    V = lambda *shape: pltpu.VMEM(shape, F32)
    D = lambda *shape: pltpu.SemaphoreType.DMA(shape)
    scratch = [
        V(5, W, C), V(2, W, C), V(5, W1, C1), V(2, W1, C1), V(5, W2, C2), V(2, W2, C2),
        V(2, W, C), V(2, W, C), V(2, W, C), V(2, W, C), V(2, N, C), V(2, N, C),
        V(2, W, C), V(2, W, C), V(2 * SPAN, 2, N, C),
        V(2, W1, C1), V(2, W1, C1), V(2, N // 2, C1), V(SPAN, 2, W1, C1), V(2, W1, C1),
        V(SPAN + 1, 2, W1, C1), V(2, 2, W1, C1), V(2, W2, C2), V(2, W2, C2), V(2, W2, C2), V(2, W2, C2),
        V(C, C1), V(C1, C),
        D(7), D(2, 5), D(2, 5), D(3, 3), D(3), D(2), D(2), D(3), D(3), D(2), D(2),
        D(GROUP, 3), D(3), D(2, 2 * GROUP - 1, 3), D(SPAN, 3), D(3), D(3), D(2), D(2), D(2 * SPAN),
    ]

    def body(*refs):
        kernel(T, S, *refs)

    return pl.pallas_call(
        body,
        out_shape=jax.ShapeDtypeStruct(guess.shape, F32),
        in_specs=[pl.BlockSpec(memory_space=pl.ANY)] * 6,
        out_specs=pl.BlockSpec(memory_space=pl.ANY),
        scratch_shapes=scratch,
        compiler_params=pltpu.CompilerParams(
            collective_id=0, has_side_effects=True, vmem_limit_bytes=48 * 1024 * 1024
        ),
    )(initial, guess, kappa, feed, kill, react)


def solution(mesh):
    T, S = mesh.shape["tm"], mesh.shape["space"]
    in_specs = (
        P(None, "space", None),
        P("tm", None, "space", None),
        P(None, "space", None),
        P("space", None),
        P("space", None),
        P("space", None),
    )
    out_specs = P("tm", None, "space", None)

    def run(*args):
        return local(T, S, *args)

    return jax.shard_map(run, mesh=mesh, in_specs=in_specs, out_specs=out_specs, check_vma=False)
```

time: 511 us -> 50.2 us (0.10)
  the two profiles are of different devices: /device:TPU:8 before, /device:TPU:20 now
where the time goes in v1:
time: 50.2 us; the launch traced here: 49.9 us
  Pallas kernels  42.6 us (85%)
  local copies, waits for them, and re-layouts  7.24 us (14%)
    pallas_call x1, Pallas kernels, local(): pl.pallas_call(body, out_shape=jax.ShapeDtypeStruct(guess.shape, F32), in...  42.6 us
    unnamed x13, local copies, waits for them, and re-layouts  7.24 us

profile of v1, /device:TPU:20, one launch (start us, length us, event | category | flops | bytes accessed | tf_op | source)
XLA Modules:
  0.0 49.9 jit_solution(15260917425171801287)
XLA Ops:
  0.0 0.0 copy-start
  0.0 1.6 %copy-done = f32[16,2,32,512]{3,2,1,0:T(8,128)S(1)} copy-done((f32[16,2,32,512]{3,2,1,0:T(8,128)S(1)}, f32[16,2,32,512]{3,2,1,0:T(8,128)}, u32[]{:S(2)}) %copy-start) | copy-done | bytes 2097176
  1.6 0.0 copy-start.1
  1.6 0.9 %copy-done.1 = f32[2,32,512]{2,1,0:T(8,128)S(1)} copy-done((f32[2,32,512]{2,1,0:T(8,128)S(1)}, f32[2,32,512]{2,1,0:T(8,128)}, u32[]{:S(2)}) %copy-start.1) | copy-done | bytes 131096
  2.5 0.0 copy-start.2
  2.5 0.9 %copy-done.2 = f32[2,32,512]{2,1,0:T(8,128)S(1)} copy-done((f32[2,32,512]{2,1,0:T(8,128)S(1)}, f32[2,32,512]{2,1,0:T(8,128)}, u32[]{:S(2)}) %copy-start.2) | copy-done | bytes 131096
  3.4 0.0 copy-start.3
  3.4 0.8 %copy-done.3 = f32[32,512]{1,0:T(8,128)S(1)} copy-done((f32[32,512]{1,0:T(8,128)S(1)}, f32[32,512]{1,0:T(8,128)}, u32[]{:S(2)}) %copy-start.3) | copy-done | bytes 65560
  4.2 0.0 copy-start.4
  4.2 0.8 %copy-done.4 = f32[32,512]{1,0:T(8,128)S(1)} copy-done((f32[32,512]{1,0:T(8,128)S(1)}, f32[32,512]{1,0:T(8,128)}, u32[]{:S(2)}) %copy-start.4) | copy-done | bytes 65560
  5.1 0.0 copy-start.5
  5.1 0.8 %copy-done.5 = f32[32,512]{1,0:T(8,128)S(1)} copy-done((f32[32,512]{1,0:T(8,128)S(1)}, f32[32,512]{1,0:T(8,128)}, u32[]{:S(2)}) %copy-start.5) | copy-done | bytes 65560
  5.9 42.6 %shard_map.64 = f32[16,2,32,512]{3,2,1,0:T(8,128)S(1)} custom-call(f32[2,32,512]{2,1,0:T(8,128)S(1)} %copy-done.1, f32[16,2,32,512]{3,2,1,0:T(8,128)S(1)} %copy-done, f32[2,32,512]{2,1,0:T(8,128)S(1)} %copy-done.2, f32[32,512]{1,0:T(8,128)S(1)} %copy-done.3, f32[32,512]{1,0:T(8,128)S(1)} %copy-done.4, f32[32,512]{1,0:T(8,128)S(1)} %copy-done.5), custom_call_target="tpu_custom_call" | custom-call | tf_op jit(solution)/shard_map/pallas_call | solution.py:460
  48.6 1.3 %copy.8 = f32[16,2,32,512]{3,2,1,0:T(8,128)} copy(f32[16,2,32,512]{3,2,1,0:T(8,128)S(1)} %shard_map.64) | data formatting | bytes 4194304
Async XLA Ops:
  0.0 1.6 %copy-start = (f32[16,2,32,512]{3,2,1,0:T(8,128)S(1)}, f32[16,2,32,512]{3,2,1,0:T(8,128)}, u32[]{:S(2)}) copy-start(f32[16,2,32,512]{3,2,1,0:T(8,128)} %refs_1_.1) | copy-start | bytes 6291460
  1.6 0.9 %copy-start.1 = (f32[2,32,512]{2,1,0:T(8,128)S(1)}, f32[2,32,512]{2,1,0:T(8,128)}, u32[]{:S(2)}) copy-start(f32[2,32,512]{2,1,0:T(8,128)} %refs_0_.1) | copy-start | bytes 393220
  2.5 0.9 %copy-start.2 = (f32[2,32,512]{2,1,0:T(8,128)S(1)}, f32[2,32,512]{2,1,0:T(8,128)}, u32[]{:S(2)}) copy-start(f32[2,32,512]{2,1,0:T(8,128)} %refs_2_.1) | copy-start | bytes 393220
  3.4 0.8 %copy-start.3 = (f32[32,512]{1,0:T(8,128)S(1)}, f32[32,512]{1,0:T(8,128)}, u32[]{:S(2)}) copy-start(f32[32,512]{1,0:T(8,128)} %refs_3_.1) | copy-start | bytes 196612
  4.2 0.8 %copy-start.4 = (f32[32,512]{1,0:T(8,128)S(1)}, f32[32,512]{1,0:T(8,128)}, u32[]{:S(2)}) copy-start(f32[32,512]{1,0:T(8,128)} %refs_4_.1) | copy-start | bytes 196612
  5.1 0.8 %copy-start.5 = (f32[32,512]{1,0:T(8,128)S(1)}, f32[32,512]{1,0:T(8,128)}, u32[]{:S(2)}) copy-start(f32[32,512]{1,0:T(8,128)} %refs_5_.1) | copy-start | bytes 196612

commit v2 on v1

v2 whole, which is shorter than its diff:
```python
import jax
import jax.numpy as jnp
from jax import lax
from jax.experimental import pallas as pl
from jax.experimental.pallas import tpu as pltpu
from jax.sharding import PartitionSpec as P

SPAN = 8
H = 8
GROUP = SPAN // 2
MESH = pl.DeviceIdType.MESH
F32 = jnp.float32


def phi(src, coef, quad, first, last, total, emit):
    cols = src.shape[-1]
    lane = lax.broadcasted_iota(jnp.int32, (8, cols), 1)
    row = lax.broadcasted_iota(jnp.int32, (8, cols), 0)
    cache = {}

    def load(b, sp):
        b = b % total
        if (b, sp) not in cache:
            x = src[sp, b * 8 : b * 8 + 8, :]
            cache[b, sp] = (x, pltpu.roll(x, 1, 0), pltpu.roll(x, 7, 0))
        return cache[b, sp]

    for blk in range(first, last):
        rows = slice(blk * 8, blk * 8 + 8)
        x = []
        around = []
        for sp in range(2):
            v, down, up = load(blk, sp)
            above = jnp.where(row == 0, load(blk - 1, sp)[1], down)
            below = jnp.where(row == 7, load(blk + 1, sp)[2], up)
            left = jnp.where(lane == 0, 0.0, pltpu.roll(v, 1, 1))
            right = jnp.where(lane == cols - 1, 0.0, pltpu.roll(v, cols - 1, 1))
            x.append(v)
            around.append((above + below) + (left + right))
        c = coef[4, rows, :] * x[0] * (x[1] * x[1])
        emit(blk, 0, quad[0, rows, :] * x[0] + coef[0, rows, :] * around[0] + (coef[2, rows, :] - c))
        emit(blk, 1, quad[1, rows, :] * x[1] + coef[1, rows, :] * around[1] + c)


def into(dst, shift=0):
    def emit(b, sp, value):
        dst[sp, b * 8 + shift : b * 8 + shift + 8, :] = value

    return emit


def pieces(x):
    t = x * 65537.0
    a = t - (t - x)
    r = x - a
    t = r * 65537.0
    b = t - (t - r)
    return [a, b, r - b]


def times(x, matrix):
    n = x.shape[0]
    y = jnp.dot(jnp.concatenate(pieces(x), 0), matrix, preferred_element_type=F32)
    return y[:n] + y[n : 2 * n] + y[2 * n :]


def row_matrix(out_rows, in_rows, shift, expand):
    i = lax.broadcasted_iota(jnp.int32, (out_rows, in_rows), 0)
    j = lax.broadcasted_iota(jnp.int32, (out_rows, in_rows), 1)
    d = (i - 2 * j if expand else j - 2 * i) + shift
    m = jnp.where((d == 0) | (d == 1), 1.0 if expand else 0.25, 0.0)
    return jnp.concatenate([m, m, m], 1)


def rows_times(matrix, x):
    return jnp.dot(matrix, jnp.concatenate(pieces(x), 0), preferred_element_type=F32)


def coarsen(xs, wide, cmat):
    rows, cols = xs[0].shape
    out_rows = (rows - 2 * H) // 2 + 2 * H if wide else rows // 2
    m = row_matrix(out_rows, rows, H if wide else 0, False)
    y = times(jnp.concatenate(xs, 0), cmat[0:cols, 0 : cols // 2])
    return [rows_times(m, y[k * rows : (k + 1) * rows]) for k in range(len(xs))]


def refine(xs, emat):
    rows, cols = xs[0].shape
    out_rows = (rows - 2 * H) * 2 + 2 * H
    m = row_matrix(out_rows, rows, H, True)
    y = jnp.concatenate([rows_times(m, x) for x in xs], 0)
    z = times(y, emat[0:cols, 0 : 2 * cols])
    return [z[k * out_rows : (k + 1) * out_rows] for k in range(len(xs))]


def kernel(
    T, S,
    initial, guess, kappa, feed, kill, react, out,
    cf, q0, c1, q1, c2, q2, ga, gb, ca, cb, cc, st0, st1, outbuf,
    wa, wb, wc, gs, vs, vv, ps, pr, ei, eo, zz, zy, cmat, emat,
    s_loc, r_cf, r_gb, r_ga, r_c1, r_ca, r_cb, r_vs, r_gs, r_fw, r_e, r_d, s_out, s_send,
):
    t = lax.axis_index("tm")
    s = lax.axis_index("space")
    m = lax.rem(t, GROUP)
    base = t - m
    N = cf.shape[1] - 2 * H
    N1 = c1.shape[1] - 2 * H
    N2 = ei.shape[1] - 2 * H
    has = {-1: s > 0, 1: s < S - 1}
    opening = t == 0
    further = t < T - 1
    first = m == 0
    follows = base > 0
    leads = t + GROUP < T
    partner = m + 1 - 2 * lax.rem(m, 2)
    across = lax.rem(m + 2, GROUP)
    sends = []
    number = [0]

    def edge(n, ds):
        if ds == -1:
            return slice(0, H), slice(n + H, n + 2 * H)
        if ds == 1:
            return slice(n - H, n), slice(0, H)
        return slice(0, n), slice(H, n + H)

    def shift(sl, by):
        return slice(sl.start + by, sl.stop + by)

    def begin(cond, copies):
        made = []
        for src, dst, rsem, tt, ss in copies:
            made.append(pltpu.make_async_remote_copy(
                src_ref=src, dst_ref=dst, send_sem=s_send.at[number[0]], recv_sem=rsem,
                device_id=(tt, ss), device_id_type=MESH,
            ))
            number[0] += 1

        def go():
            for c in made:
                c.start()

        if cond is None:
            go()
        else:
            pl.when(cond)(go)
        sends.append((cond, made))

    def arrive(cond, waits):
        def go():
            for dst, rsem in waits:
                pltpu.make_async_copy(dst, dst, rsem).wait()

        if cond is None:
            go()
        else:
            pl.when(cond)(go)

    mid = slice(H, N + H)
    inner = slice(H, N1 + H)
    core = slice(H, N2 + H)
    local = [
        pltpu.make_async_copy(guess.at[SPAN - 1], gb.at[:, mid], s_loc.at[0]),
        pltpu.make_async_copy(kappa, cf.at[0:2, mid], s_loc.at[1]),
        pltpu.make_async_copy(feed, cf.at[2, mid], s_loc.at[2]),
        pltpu.make_async_copy(kill, cf.at[3, mid], s_loc.at[3]),
        pltpu.make_async_copy(react, cf.at[4, mid], s_loc.at[4]),
    ]
    for c in local:
        c.start()
    opened = [
        pltpu.make_async_copy(initial, ga.at[:, mid], s_loc.at[5]),
        pltpu.make_async_copy(initial, ca.at[:, mid], s_loc.at[6]),
    ]

    @pl.when(opening)
    def _():
        for c in opened:
            c.start()

    for ds in (-1, 1):
        @pl.when(jnp.logical_not(has[ds]))
        def _():
            for ref, n in ((cf, N), (ga, N), (gb, N), (ca, N), (cb, N), (c1, N1), (vs, N1)):
                rows = slice(0, H) if ds == -1 else slice(n + H, n + 2 * H)
                ref[:, rows, :] = jnp.zeros((ref.shape[0], H, ref.shape[2]), F32)
            rows = slice(0, H) if ds == -1 else slice(N1 + H, N1 + 2 * H)
            gs[:, :, rows, :] = jnp.zeros((SPAN, 2, H, gs.shape[3]), F32)
            pr[(1 - ds) // 2] = jnp.zeros(pr.shape[1:], F32)
            rows = slice(0, H) if ds == -1 else slice(N2 + H, N2 + 2 * H)
            ei[:, rows, :] = jnp.zeros((2, H, ei.shape[2]), F32)

    @pl.when(base == 0)
    def _():
        ei[...] = jnp.zeros(ei.shape, F32)

    barrier = pltpu.get_barrier_semaphore()
    count = jnp.int32(0)
    known = []
    for dt in (-GROUP, -1, 0, 1, GROUP):
        known.append((t + dt, (t + dt >= 0) & (t + dt < T), dt == 0))
    known.append((base + across, t >= 0, False))
    far = GROUP - 1 - m
    known.append((base + far, (m == 0) | (m == GROUP - 1), False))
    for other, there, own in known:
        for ds in (-1, 0, 1):
            if own and ds == 0:
                continue
            cond = there & has[ds] if ds else there

            @pl.when(cond)
            def _():
                pl.semaphore_signal(barrier, inc=1, device_id=(other, s + ds), device_id_type=MESH)

            count = count + cond.astype(jnp.int32)

    pl.semaphore_wait(barrier, count)

    for ds in (-1, 1):
        src, dst = edge(N, ds)
        k = (ds + 1) // 2
        begin(has[ds], [
            (guess.at[SPAN - 1, :, src], gb.at[:, dst], r_gb.at[k], t, s + ds),
            (kappa.at[:, src], cf.at[0:2, dst], r_cf.at[k, 0], t, s + ds),
            (feed.at[src], cf.at[2, dst], r_cf.at[k, 1], t, s + ds),
            (kill.at[src], cf.at[3, dst], r_cf.at[k, 2], t, s + ds),
            (react.at[src], cf.at[4, dst], r_cf.at[k, 3], t, s + ds),
        ])
    begin(further, [(guess.at[2 * SPAN - 1], ga.at[:, mid], r_ga.at[1], t + 1, s)])

    ii = lax.broadcasted_iota(jnp.int32, cmat.shape, 0) - 2 * lax.broadcasted_iota(jnp.int32, cmat.shape, 1)
    cmat[...] = jnp.where((ii == 0) | (ii == 1), 1.0, 0.0)
    jj = lax.broadcasted_iota(jnp.int32, emat.shape, 1) - 2 * lax.broadcasted_iota(jnp.int32, emat.shape, 0)
    emat[...] = jnp.where((jj == 0) | (jj == 1), 1.0, 0.0)
    eo[...] = jnp.zeros(eo.shape, F32)

    for c in local:
        c.wait()
    scale = (2.0, 2.0, 8.0, 8.0, 8.0)
    for k, x in enumerate(coarsen([cf[k, mid, :] for k in range(5)], False, cmat)):
        c1[k, inner, :] = scale[k] * x
    for k, x in enumerate(coarsen([c1[k, inner, :] for k in range(5)], False, cmat)):
        c2[k, core, :] = scale[k] * x
    q2[0, core, :] = 1.0 - c2[2, core, :] - 4.0 * c2[0, core, :]
    q2[1, core, :] = 1.0 - (c2[2, core, :] + c2[3, core, :]) - 4.0 * c2[1, core, :]

    for ds in (-1, 1):
        k = (ds + 1) // 2
        dst = edge(N, ds)[1]
        arrive(has[-ds], [
            (gb.at[:, dst], r_gb.at[k]),
            (cf.at[0:2, dst], r_cf.at[k, 0]),
            (cf.at[2, dst], r_cf.at[k, 1]),
            (cf.at[3, dst], r_cf.at[k, 2]),
            (cf.at[4, dst], r_cf.at[k, 3]),
        ])
    for ds in (-1, 1):
        src, dst = edge(N, ds)
        src1, dst1 = edge(N1, ds)
        begin(further & has[ds], [
            (guess.at[2 * SPAN - 1, :, src], ga.at[:, dst], r_ga.at[ds + 1], t + 1, s + ds),
        ])
        begin(opening & has[ds], [
            (initial.at[:, src], ga.at[:, dst], r_ga.at[ds + 1], t, s + ds),
            (initial.at[:, src], ca.at[:, dst], r_ca.at[ds + 1], t, s + ds),
        ])
        begin(has[ds], [
            (c1.at[:, shift(src1, H)], c1.at[:, dst1], r_c1.at[(ds + 1) // 2], t, s + ds),
        ])

    def quads(coef, quad):
        quad[0] = 1.0 - coef[2] - 4.0 * coef[0]
        quad[1] = 1.0 - (coef[2] + coef[3]) - 4.0 * coef[1]

    quads(cf, q0)
    blocks = (N + 2 * H) // 8

    def interval(src):
        st1[...] = src[...]

        @pl.loop(0, SPAN // 2)
        def _(_):
            phi(st1, cf, q0, 0, blocks, blocks, into(st0))
            phi(st0, cf, q0, 0, blocks, blocks, into(st1))

    interval(gb)
    cc[...] = st1[:, mid, :]
    begin(further, [(cc, ca.at[:, mid], r_ca.at[1], t + 1, s)])
    for ds in (-1, 1):
        src, dst = edge(N, ds)
        begin(further & has[ds], [(cc.at[:, src], ca.at[:, dst], r_ca.at[ds + 1], t + 1, s + ds)])

    @pl.when(opening)
    def _():
        for c in opened:
            c.wait()

    arrive(jnp.logical_not(opening), [(ga.at[:, mid], r_ga.at[1])])
    for ds in (-1, 1):
        arrive(has[-ds], [(ga.at[:, edge(N, ds)[1]], r_ga.at[ds + 1])])
    interval(ga)
    cb[:, mid, :] = st1[:, mid, :]
    for ds in (-1, 1):
        src, dst = edge(N, ds)
        begin(has[ds], [(cb.at[:, shift(src, H)], cb.at[:, dst], r_cb.at[(ds + 1) // 2], t, s + ds)])

    arrive(jnp.logical_not(opening), [(ca.at[:, mid], r_ca.at[1])])
    for ds in (-1, 1):
        arrive(has[-ds], [
            (ca.at[:, edge(N, ds)[1]], r_ca.at[ds + 1]),
            (c1.at[:, edge(N1, ds)[1]], r_c1.at[(ds + 1) // 2]),
        ])
    quads(c1, q1)
    blocks1 = (N1 + 2 * H) // 8
    for k, x in enumerate(coarsen([ca[0], ca[1]], True, cmat)):
        wa[k] = x

    @pl.when(first)
    def _():
        vs[:, inner, :] = wa[:, inner, :]

    begin(first, [(wa.at[:, inner], vs.at[:, inner], r_vs.at[1], base + r, s) for r in range(1, GROUP)])
    for ds in (-1, 1):
        src, dst = edge(N1, ds)
        begin(first & has[ds], [
            (wa.at[:, shift(src, H)], vs.at[:, dst], r_vs.at[ds + 1], base + r, s + ds) for r in range(GROUP)
        ])

    def forcing(which, w, r):
        slot = 2 * m + which
        last = jnp.where(m == GROUP - 1, 1.0, 0.0) if which else None

        def emit(b, sp, value):
            rows = slice(b * 8 - H, b * 8 - H + 8)
            g = r[sp][rows] - value
            if which:
                g = g - last * wc[sp, rows, :]
            gs[slot, sp, b * 8 : b * 8 + 8, :] = g

        phi(w, c1, q1, 1, blocks1 - 1, blocks1, emit)
        begin(None, [
            (gs.at[slot, :, inner], gs.at[slot, :, inner], r_gs.at[slot, 1], base + to, s)
            for to in (across, partner)
        ])
        for ds in (-1, 1):
            src, dst = edge(N1, ds)
            begin(has[ds], [
                (gs.at[slot, :, shift(src, H)], gs.at[slot, :, dst], r_gs.at[slot, ds + 1], base + to, s + ds)
                for to in (across, partner, m)
            ])

    interval(ca)
    forcing(0, wa, coarsen([st1[0, mid, :], st1[1, mid, :]], False, cmat))
    for k, x in enumerate(coarsen([cc[0], cc[1]], False, cmat)):
        wc[k] = x
    for ds in (-1, 1):
        arrive(has[-ds], [(cb.at[:, edge(N, ds)[1]], r_cb.at[(ds + 1) // 2])])
    for k, x in enumerate(coarsen([cb[0], cb[1]], True, cmat)):
        wb[k] = x
    interval(cb)
    forcing(1, wb, coarsen([st1[0, mid, :], st1[1, mid, :]], False, cmat))

    for which in range(2):
        slot = 2 * across + which
        arrive(None, [(gs.at[slot, :, inner], r_gs.at[slot, 1])])
        for ds in (-1, 1):
            arrive(has[-ds], [(gs.at[slot, :, edge(N1, ds)[1]], r_gs.at[slot, ds + 1])])
        begin(None, [(gs.at[slot], gs.at[slot], r_fw.at[slot], base + partner, s)])

    arrive(jnp.logical_not(first), [(vs.at[:, inner], r_vs.at[1])])
    for ds in (-1, 1):
        arrive(has[-ds], [(vs.at[:, edge(N1, ds)[1]], r_vs.at[ds + 1])])
    vv[0] = vs[...]
    for sp, x in enumerate(coarsen([vs[0], vs[1]], True, cmat)):
        zz[sp] = x
    top = (N2 + 2 * H) // 8

    def emit_old(b, sp, value):
        eo[sp, b * 8 : b * 8 + 8, :] = -value

    def emit_new(b, sp, value):
        rows = slice(b * 8, b * 8 + 8)
        eo[sp, rows, :] = eo[sp, rows, :] + value

    phi(zz, c2, q2, 1, top - 1, top, emit_old)

    for which in range(2):
        slot = 2 * partner + which
        arrive(None, [(gs.at[slot, :, inner], r_gs.at[slot, 1])])
        for ds in (-1, 1):
            arrive(has[-ds], [
                (gs.at[slot, :, edge(N1, ds)[1]], r_gs.at[slot, ds + 1]),
                (gs.at[2 * m + which, :, edge(N1, ds)[1]], r_gs.at[2 * m + which, ds + 1]),
            ])
    other = lax.rem(partner + 2, GROUP)
    for which in range(2):
        slot = 2 * other + which
        arrive(None, [(gs.at[slot], r_fw.at[slot])])

    def sweep(count):
        @pl.loop(0, count)
        def _(i):
            def emit(b, sp, value):
                rows = slice(b * 8, b * 8 + 8)
                vv[i + 1, sp, rows, :] = value + gs[i, sp, rows, :]

            phi(vv.at[i], c1, q1, 0, blocks1, blocks1, emit)

    sweep(SPAN)

    r = coarsen([vv[SPAN, sp, inner, :] for sp in range(2)], False, cmat)
    arrive(follows, [(ei.at[:, core], r_e.at[1])])
    for ds in (-1, 1):
        arrive(follows & has[-ds], [(ei.at[:, edge(N2, ds)[1]], r_e.at[ds + 1])])
    for sp in range(2):
        zy[sp] = zz[sp] + ei[sp]
    phi(zy, c2, q2, 1, top - 1, top, emit_new)
    for sp in range(2):
        eo[sp, core, :] = eo[sp, core, :] + r[sp]
    begin(leads, [(eo.at[:, core], ei.at[:, core], r_e.at[1], t + GROUP, s)])
    for ds in (-1, 1):
        src, dst = edge(N2, ds)
        begin(leads & has[ds], [
            (eo.at[:, shift(src, H)], ei.at[:, dst], r_e.at[ds + 1], t + GROUP, s + ds),
        ])

    p = refine([ei[0], ei[1]], emat)
    for sp in range(2):
        vv[0, sp] = vs[sp] + p[sp]
    sweep(SPAN - 1)
    da = vv[2 * m, :, inner, :] - wa[:, inner, :]
    db = vv[2 * m + 1, :, inner, :] - wb[:, inner, :]
    half = H // 2
    for sp in range(2):
        ps[0, sp] = jnp.concatenate([da[sp, 0:half], db[sp, 0:half]], 0)
        ps[1, sp] = jnp.concatenate([da[sp, N1 - half :], db[sp, N1 - half :]], 0)
    for ds in (-1, 1):
        k = (ds + 1) // 2
        begin(has[ds], [(ps.at[k], pr.at[k], r_d.at[k], t, s + ds)])

    def done(i):
        return pltpu.make_async_copy(outbuf.at[i], out.at[i], s_out.at[i])

    p = refine([eo[0], eo[1]], emat)
    for sp in range(2):
        vv[SPAN, sp, inner, :] = wc[sp] + p[sp][inner]
    zeros = jnp.zeros((H, c1.shape[2]), F32)
    tail = [
        jnp.concatenate([zeros, vv[2 * m + 2, sp, inner, :] - wc[sp], zeros], 0) for sp in range(2)
    ]
    p = refine(tail, emat)
    for sp in range(2):
        outbuf[2 * SPAN - 1, sp] = cc[sp] + p[sp][mid]
    done(2 * SPAN - 1).start()

    for ds in (-1, 1):
        k = (ds + 1) // 2
        arrive(has[-ds], [(pr.at[k], r_d.at[k])])
    zeros = jnp.zeros((half, c1.shape[2]), F32)
    delta = []
    for which, d in enumerate((da, db)):
        rows = slice(which * half, which * half + half)
        for sp in range(2):
            delta.append(jnp.concatenate([zeros, pr[1, sp, rows, :], d[sp], pr[0, sp, rows, :], zeros], 0))
    p = refine(delta, emat)
    for sp in range(2):
        st1[sp] = ca[sp] + p[sp]
        u = cb[sp] + p[2 + sp]
        gb[sp] = u
        outbuf[SPAN - 1, sp] = u[mid]
    done(SPAN - 1).start()

    def final(at):
        def step(a, b, i):
            def emit(blk, sp, value):
                b[sp, blk * 8 : blk * 8 + 8, :] = value
                if 1 <= blk < blocks - 1:
                    outbuf[i, sp, blk * 8 - H : blk * 8 - H + 8, :] = value

            phi(a, cf, q0, 0, blocks, blocks, emit)
            done(i).start()

        @pl.loop(0, 3)
        def _(k):
            step(st1, st0, at + 2 * k)
            step(st0, st1, at + 1 + 2 * k)

        step(st1, st0, at + 6)

    final(0)
    st1[...] = gb[...]
    final(SPAN)
    for i in range(2 * SPAN):
        done(i).wait()
    for cond, made in sends:
        def settle():
            for c in made:
                c.wait_send()

        if cond is None:
            settle()
        else:
            pl.when(cond)(settle)


def local(T, S, initial, guess, kappa, feed, kill, react):
    _, N, C = initial.shape
    W, W1, W2 = N + 2 * H, N // 2 + 2 * H, N // 4 + 2 * H
    C1, C2 = C // 2, C // 4
    V = lambda *shape: pltpu.VMEM(shape, F32)
    D = lambda *shape: pltpu.SemaphoreType.DMA(shape)
    scratch = [
        V(5, W, C), V(2, W, C), V(5, W1, C1), V(2, W1, C1), V(5, W2, C2), V(2, W2, C2),
        V(2, W, C), V(2, W, C), V(2, W, C), V(2, W, C), V(2, N, C),
        V(2, W, C), V(2, W, C), V(2 * SPAN, 2, N, C),
        V(2, W1, C1), V(2, W1, C1), V(2, N // 2, C1), V(SPAN, 2, W1, C1), V(2, W1, C1),
        V(SPAN + 1, 2, W1, C1), V(2, 2, H, C1), V(2, 2, H, C1), V(2, W2, C2), V(2, W2, C2),
        V(2, W2, C2), V(2, W2, C2), V(C, C1), V(C1, C),
        D(7), D(2, 4), D(2), D(3), D(2), D(3), D(2), D(3), D(SPAN, 3), D(SPAN), D(3), D(2),
        D(2 * SPAN), D(96),
    ]

    def body(*refs):
        kernel(T, S, *refs)

    return pl.pallas_call(
        body,
        out_shape=jax.ShapeDtypeStruct(guess.shape, F32),
        in_specs=[pl.BlockSpec(memory_space=pl.ANY)] * 6,
        out_specs=pl.BlockSpec(memory_space=pl.ANY),
        scratch_shapes=scratch,
        compiler_params=pltpu.CompilerParams(
            collective_id=0, has_side_effects=True, vmem_limit_bytes=64 * 1024 * 1024
        ),
    )(initial, guess, kappa, feed, kill, react)


def solution(mesh):
    T, S = mesh.shape["tm"], mesh.shape["space"]
    in_specs = (
        P(None, "space", None),
        P("tm", None, "space", None),
        P(None, "space", None),
        P("space", None),
        P("space", None),
        P("space", None),
    )
    out_specs = P("tm", None, "space", None)

    def run(*args):
        return local(T, S, *args)

    return jax.shard_map(run, mesh=mesh, in_specs=in_specs, out_specs=out_specs, check_vma=False)
```

time: 50.2 us -> 44.3 us (0.88)
  local copies, waits for them, and re-layouts: 7.24 us -> 3.19 us
  Pallas kernels: 42.6 us -> 41 us
    unnamed x13 -> x1, local copies, waits for them, and re-layouts: 7.24 us -> 3.19 us
    pallas_call x1, Pallas kernels: 42.6 us -> 41 us  [local(): pl.pallas_call(body, out_shape=jax.ShapeDtypeStruct(guess.shape, F32), in...]
where the time goes in v2:
time: 44.3 us; the launch traced here: 44.2 us
  Pallas kernels  41 us (93%)
  local copies, waits for them, and re-layouts  3.19 us (7%)
    pallas_call x1, Pallas kernels, local(): pl.pallas_call(body, out_shape=jax.ShapeDtypeStruct(guess.shape, F32), in...  41 us
    unnamed x1, local copies, waits for them, and re-layouts  3.19 us

profile of v2, /device:TPU:20, one launch (start us, length us, event | category | flops | bytes accessed | tf_op | source)
XLA Modules:
  0.0 44.2 jit_solution(16834584484776854482)
XLA Ops:
  0.0 41.0 %shard_map.64 = f32[16,2,32,512]{3,2,1,0:T(8,128)} custom-call(f32[2,32,512]{2,1,0:T(8,128)} %refs_0_.1, f32[16,2,32,512]{3,2,1,0:T(8,128)} %refs_1_.1, f32[2,32,512]{2,1,0:T(8,128)} %refs_2_.1, f32[32,512]{1,0:T(8,128)} %refs_3_.1, f32[32,512]{1,0:T(8,128)} %refs_4_.1, f32[32,512]{1,0:T(8,128)} %refs_5_.1), custom_call_target="tpu_custom_call" | custom-call | tf_op jit(solution)/shard_map/pallas_call | solution.py:527
  41.0 3.2 %copy.8 = f32[16,2,32,512]{3,2,1,0:T(8,128)} copy(f32[16,2,32,512]{3,2,1,0:T(8,128)} %shard_map.64) | data formatting | bytes 4194304

commit v3 on v2

--- a/solution.py
+++ b/solution.py
@@ -10,94 +10,110 @@
 GROUP = SPAN // 2
 MESH = pl.DeviceIdType.MESH
 F32 = jnp.float32
-
-
-def phi(src, coef, quad, first, last, total, emit):
-    cols = src.shape[-1]
-    lane = lax.broadcasted_iota(jnp.int32, (8, cols), 1)
-    row = lax.broadcasted_iota(jnp.int32, (8, cols), 0)
+BF16 = jnp.bfloat16
+L = 128
+
+
+def phi(jobs, coef, quad, first, last, total):
+    tiles = jobs[0][0].shape[-1] // L
+    lane = lax.broadcasted_iota(jnp.int32, (8, L), 1)
+    row = lax.broadcasted_iota(jnp.int32, (8, L), 0)
+    low, high = lane == 0, lane == L - 1
+    top, bottom = row == 0, row == 7
     cache = {}
 
-    def load(b, sp):
-        b = b % total
-        if (b, sp) not in cache:
-            x = src[sp, b * 8 : b * 8 + 8, :]
-            cache[b, sp] = (x, pltpu.roll(x, 1, 0), pltpu.roll(x, 7, 0))
-        return cache[b, sp]
+    def load(job, b, sp, c):
+        key = (job, b, sp, c)
+        if key not in cache:
+            x = jobs[job][0][sp, b * 8 : b * 8 + 8, c * L : c * L + L]
+            cache[key] = (x, pltpu.roll(x, 1, 0), pltpu.roll(x, 7, 0), pltpu.roll(x, 1, 1), pltpu.roll(x, L - 1, 1))
+        return cache[key]
 
     for blk in range(first, last):
         rows = slice(blk * 8, blk * 8 + 8)
-        x = []
-        around = []
-        for sp in range(2):
-            v, down, up = load(blk, sp)
-            above = jnp.where(row == 0, load(blk - 1, sp)[1], down)
-            below = jnp.where(row == 7, load(blk + 1, sp)[2], up)
-            left = jnp.where(lane == 0, 0.0, pltpu.roll(v, 1, 1))
-            right = jnp.where(lane == cols - 1, 0.0, pltpu.roll(v, cols - 1, 1))
-            x.append(v)
-            around.append((above + below) + (left + right))
-        c = coef[4, rows, :] * x[0] * (x[1] * x[1])
-        emit(blk, 0, quad[0, rows, :] * x[0] + coef[0, rows, :] * around[0] + (coef[2, rows, :] - c))
-        emit(blk, 1, quad[1, rows, :] * x[1] + coef[1, rows, :] * around[1] + c)
-
-
-def into(dst, shift=0):
-    def emit(b, sp, value):
-        dst[sp, b * 8 + shift : b * 8 + shift + 8, :] = value
+        for c in range(tiles):
+            cols = slice(c * L, c * L + L)
+            k = [coef[i, rows, cols] for i in (0, 1, 2, 4)]
+            q = [quad[i, rows, cols] for i in (0, 1)]
+            for job, (_, emit) in enumerate(jobs):
+                x, around = [], []
+                for sp in range(2):
+                    v, above, below, left, right = load(job, blk, sp, c)
+                    if blk > 0:
+                        above = jnp.where(top, load(job, blk - 1, sp, c)[1], above)
+                    if blk < total - 1:
+                        below = jnp.where(bottom, load(job, blk + 1, sp, c)[2], below)
+                    left = jnp.where(low, load(job, blk, sp, c - 1)[3] if c > 0 else 0.0, left)
+                    right = jnp.where(high, load(job, blk, sp, c + 1)[4] if c < tiles - 1 else 0.0, right)
+                    x.append(v)
+                    around.append((above + below) + (left + right))
+                r = k[3] * x[0] * (x[1] * x[1])
+                emit(0, rows, cols, q[0] * x[0] + k[0] * around[0] + (k[2] - r))
+                emit(1, rows, cols, q[1] * x[1] + k[1] * around[1] + r)
+
+
+def into(dst):
+    def emit(sp, rows, cols, value):
+        dst[sp, rows, cols] = value
 
     return emit
-
-
-def pieces(x):
-    t = x * 65537.0
-    a = t - (t - x)
-    r = x - a
-    t = r * 65537.0
-    b = t - (t - r)
-    return [a, b, r - b]
 
 
 def times(x, matrix):
     n = x.shape[0]
-    y = jnp.dot(jnp.concatenate(pieces(x), 0), matrix, preferred_element_type=F32)
+    a = x.astype(BF16)
+    r = x - a.astype(F32)
+    b = r.astype(BF16)
+    c = (r - b.astype(F32)).astype(BF16)
+    y = jnp.dot(jnp.concatenate([a, b, c], 0), matrix, preferred_element_type=F32)
     return y[:n] + y[n : 2 * n] + y[2 * n :]
 
 
-def row_matrix(out_rows, in_rows, shift, expand):
-    i = lax.broadcasted_iota(jnp.int32, (out_rows, in_rows), 0)
-    j = lax.broadcasted_iota(jnp.int32, (out_rows, in_rows), 1)
-    d = (i - 2 * j if expand else j - 2 * i) + shift
-    m = jnp.where((d == 0) | (d == 1), 1.0 if expand else 0.25, 0.0)
-    return jnp.concatenate([m, m, m], 1)
-
-
-def rows_times(matrix, x):
-    return jnp.dot(matrix, jnp.concatenate(pieces(x), 0), preferred_element_type=F32)
-
-
-def coarsen(xs, wide, cmat):
+def coarsen(xs, wide, cmat, scr):
     rows, cols = xs[0].shape
-    out_rows = (rows - 2 * H) // 2 + 2 * H if wide else rows // 2
-    m = row_matrix(out_rows, rows, H if wide else 0, False)
+    pad = H if wide else 0
+    span = rows + 2 * pad
     y = times(jnp.concatenate(xs, 0), cmat[0:cols, 0 : cols // 2])
-    return [rows_times(m, y[k * rows : (k + 1) * rows]) for k in range(len(xs))]
-
-
-def refine(xs, emat):
+    tiles = cols // 2 // L
+    for k in range(len(xs)):
+        for c in range(tiles):
+            at = k * span + pad
+            scr[c, at : at + rows, :] = y[k * rows : (k + 1) * rows, c * L : c * L + L]
+            if pad:
+                scr[c, at - pad : at, :] = jnp.zeros((pad, L), F32)
+                scr[c, at + rows : at + rows + pad, :] = jnp.zeros((pad, L), F32)
+    out = []
+    for k in range(len(xs)):
+        parts = [
+            scr[c, pl.ds(k * span, span // 2, stride=2), :] + scr[c, pl.ds(k * span + 1, span // 2, stride=2), :]
+            for c in range(tiles)
+        ]
+        out.append(0.25 * (jnp.concatenate(parts, 1) if tiles > 1 else parts[0]))
+    return out
+
+
+def refine(xs, emat, scr):
     rows, cols = xs[0].shape
-    out_rows = (rows - 2 * H) * 2 + 2 * H
-    m = row_matrix(out_rows, rows, H, True)
-    y = jnp.concatenate([rows_times(m, x) for x in xs], 0)
-    z = times(y, emat[0:cols, 0 : 2 * cols])
-    return [z[k * out_rows : (k + 1) * out_rows] for k in range(len(xs))]
+    tiles = cols // L
+    span = 2 * rows
+    for k, x in enumerate(xs):
+        for c in range(tiles):
+            for d in range(2):
+                scr[c, pl.ds(k * span + d, rows, stride=2), :] = x[:, c * L : c * L + L]
+    ys = []
+    for k in range(len(xs)):
+        parts = [scr[c, k * span + H : (k + 1) * span - H, :] for c in range(tiles)]
+        ys.append(jnp.concatenate(parts, 1) if tiles > 1 else parts[0])
+    z = times(jnp.concatenate(ys, 0), emat[0:cols, 0 : 2 * cols])
+    n = span - 2 * H
+    return [z[k * n : (k + 1) * n] for k in range(len(xs))]
 
 
 def kernel(
     T, S,
     initial, guess, kappa, feed, kill, react, out,
     cf, q0, c1, q1, c2, q2, ga, gb, ca, cb, cc, st0, st1, outbuf,
-    wa, wb, wc, gs, vs, vv, ps, pr, ei, eo, zz, zy, cmat, emat,
+    wa, wb, wc, gs, vs, vv, ps, pr, ei, eo, zz, zy, cmat, emat, scr,
     s_loc, r_cf, r_gb, r_ga, r_c1, r_ca, r_cb, r_vs, r_gs, r_fw, r_e, r_d, s_out, s_send,
 ):
     t = lax.axis_index("tm")
@@ -230,17 +246,17 @@
     begin(further, [(guess.at[2 * SPAN - 1], ga.at[:, mid], r_ga.at[1], t + 1, s)])
 
     ii = lax.broadcasted_iota(jnp.int32, cmat.shape, 0) - 2 * lax.broadcasted_iota(jnp.int32, cmat.shape, 1)
-    cmat[...] = jnp.where((ii == 0) | (ii == 1), 1.0, 0.0)
+    cmat[...] = jnp.where((ii == 0) | (ii == 1), 1.0, 0.0).astype(BF16)
     jj = lax.broadcasted_iota(jnp.int32, emat.shape, 1) - 2 * lax.broadcasted_iota(jnp.int32, emat.shape, 0)
-    emat[...] = jnp.where((jj == 0) | (jj == 1), 1.0, 0.0)
+    emat[...] = jnp.where((jj == 0) | (jj == 1), 1.0, 0.0).astype(BF16)
     eo[...] = jnp.zeros(eo.shape, F32)
 
     for c in local:
         c.wait()
     scale = (2.0, 2.0, 8.0, 8.0, 8.0)
-    for k, x in enumerate(coarsen([cf[k, mid, :] for k in range(5)], False, cmat)):
+    for k, x in enumerate(coarsen([cf[k, mid, :] for k in range(5)], False, cmat, scr)):
         c1[k, inner, :] = scale[k] * x
-    for k, x in enumerate(coarsen([c1[k, inner, :] for k in range(5)], False, cmat)):
+    for k, x in enumerate(coarsen([c1[k, inner, :] for k in range(5)], False, cmat, scr)):
         c2[k, core, :] = scale[k] * x
     q2[0, core, :] = 1.0 - c2[2, core, :] - 4.0 * c2[0, core, :]
     q2[1, core, :] = 1.0 - (c2[2, core, :] + c2[3, core, :]) - 4.0 * c2[1, core, :]
@@ -281,8 +297,8 @@
 
         @pl.loop(0, SPAN // 2)
         def _(_):
-            phi(st1, cf, q0, 0, blocks, blocks, into(st0))
-            phi(st0, cf, q0, 0, blocks, blocks, into(st1))
+            phi([(st1, into(st0))], cf, q0, 0, blocks, blocks)
+            phi([(st0, into(st1))], cf, q0, 0, blocks, blocks)
 
     interval(gb)
     cc[...] = st1[:, mid, :]
@@ -313,7 +329,7 @@
         ])
     quads(c1, q1)
     blocks1 = (N1 + 2 * H) // 8
-    for k, x in enumerate(coarsen([ca[0], ca[1]], True, cmat)):
+    for k, x in enumerate(coarsen([ca[0], ca[1]], True, cmat, scr)):
         wa[k] = x
 
     @pl.when(first)
@@ -331,14 +347,14 @@
         slot = 2 * m + which
         last = jnp.where(m == GROUP - 1, 1.0, 0.0) if which else None
 
-        def emit(b, sp, value):
-            rows = slice(b * 8 - H, b * 8 - H + 8)
-            g = r[sp][rows] - value
+        def emit(sp, rows, cols, value):
+            own = shift(rows, -H)
+            g = r[sp][own, cols] - value
             if which:
-                g = g - last * wc[sp, rows, :]
-            gs[slot, sp, b * 8 : b * 8 + 8, :] = g
-
-        phi(w, c1, q1, 1, blocks1 - 1, blocks1, emit)
+                g = g - last * wc[sp, own, cols]
+            gs[slot, sp, rows, cols] = g
+
+        phi([(w, emit)], c1, q1, 1, blocks1 - 1, blocks1)
         begin(None, [
             (gs.at[slot, :, inner], gs.at[slot, :, inner], r_gs.at[slot, 1], base + to, s)
             for to in (across, partner)
@@ -351,15 +367,15 @@
             ])
 
     interval(ca)
-    forcing(0, wa, coarsen([st1[0, mid, :], st1[1, mid, :]], False, cmat))
-    for k, x in enumerate(coarsen([cc[0], cc[1]], False, cmat)):
+    forcing(0, wa, coarsen([st1[0, mid, :], st1[1, mid, :]], False, cmat, scr))
+    for k, x in enumerate(coarsen([cc[0], cc[1]], False, cmat, scr)):
         wc[k] = x
     for ds in (-1, 1):
         arrive(has[-ds], [(cb.at[:, edge(N, ds)[1]], r_cb.at[(ds + 1) // 2])])
-    for k, x in enumerate(coarsen([cb[0], cb[1]], True, cmat)):
+    for k, x in enumerate(coarsen([cb[0], cb[1]], True, cmat, scr)):
         wb[k] = x
     interval(cb)
-    forcing(1, wb, coarsen([st1[0, mid, :], st1[1, mid, :]], False, cmat))
+    forcing(1, wb, coarsen([st1[0, mid, :], st1[1, mid, :]], False, cmat, scr))
 
     for which in range(2):
         slot = 2 * across + which
@@ -372,18 +388,17 @@
     for ds in (-1, 1):
         arrive(has[-ds], [(vs.at[:, edge(N1, ds)[1]], r_vs.at[ds + 1])])
     vv[0] = vs[...]
-    for sp, x in enumerate(coarsen([vs[0], vs[1]], True, cmat)):
+    for sp, x in enumerate(coarsen([vs[0], vs[1]], True, cmat, scr)):
         zz[sp] = x
     top = (N2 + 2 * H) // 8
 
-    def emit_old(b, sp, value):
-        eo[sp, b * 8 : b * 8 + 8, :] = -value
-
-    def emit_new(b, sp, value):
-        rows = slice(b * 8, b * 8 + 8)
-        eo[sp, rows, :] = eo[sp, rows, :] + value
-
-    phi(zz, c2, q2, 1, top - 1, top, emit_old)
+    def emit_old(sp, rows, cols, value):
+        eo[sp, rows, cols] = -value
+
+    def emit_new(sp, rows, cols, value):
+        eo[sp, rows, cols] = eo[sp, rows, cols] + value
+
+    phi([(zz, emit_old)], c2, q2, 1, top - 1, top)
 
     for which in range(2):
         slot = 2 * partner + which
@@ -401,21 +416,20 @@
     def sweep(count):
         @pl.loop(0, count)
         def _(i):
-            def emit(b, sp, value):
-                rows = slice(b * 8, b * 8 + 8)
-                vv[i + 1, sp, rows, :] = value + gs[i, sp, rows, :]
-
-            phi(vv.at[i], c1, q1, 0, blocks1, blocks1, emit)
+            def emit(sp, rows, cols, value):
+                vv[i + 1, sp, rows, cols] = value + gs[i, sp, rows, cols]
+
+            phi([(vv.at[i], emit)], c1, q1, 0, blocks1, blocks1)
 
     sweep(SPAN)
 
-    r = coarsen([vv[SPAN, sp, inner, :] for sp in range(2)], False, cmat)
+    r = coarsen([vv[SPAN, sp, inner, :] for sp in range(2)], False, cmat, scr)
     arrive(follows, [(ei.at[:, core], r_e.at[1])])
     for ds in (-1, 1):
         arrive(follows & has[-ds], [(ei.at[:, edge(N2, ds)[1]], r_e.at[ds + 1])])
     for sp in range(2):
         zy[sp] = zz[sp] + ei[sp]
-    phi(zy, c2, q2, 1, top - 1, top, emit_new)
+    phi([(zy, emit_new)], c2, q2, 1, top - 1, top)
     for sp in range(2):
         eo[sp, core, :] = eo[sp, core, :] + r[sp]
     begin(leads, [(eo.at[:, core], ei.at[:, core], r_e.at[1], t + GROUP, s)])
@@ -425,7 +439,7 @@
             (eo.at[:, shift(src, H)], ei.at[:, dst], r_e.at[ds + 1], t + GROUP, s + ds),
         ])
 
-    p = refine([ei[0], ei[1]], emat)
+    p = refine([ei[0], ei[1]], emat, scr)
     for sp in range(2):
         vv[0, sp] = vs[sp] + p[sp]
     sweep(SPAN - 1)
@@ -442,14 +456,14 @@
     def done(i):
         return pltpu.make_async_copy(outbuf.at[i], out.at[i], s_out.at[i])
 
-    p = refine([eo[0], eo[1]], emat)
+    p = refine([eo[0], eo[1]], emat, scr)
     for sp in range(2):
         vv[SPAN, sp, inner, :] = wc[sp] + p[sp][inner]
     zeros = jnp.zeros((H, c1.shape[2]), F32)
     tail = [
         jnp.concatenate([zeros, vv[2 * m + 2, sp, inner, :] - wc[sp], zeros], 0) for sp in range(2)
     ]
-    p = refine(tail, emat)
+    p = refine(tail, emat, scr)
     for sp in range(2):
         outbuf[2 * SPAN - 1, sp] = cc[sp] + p[sp][mid]
     done(2 * SPAN - 1).start()
@@ -463,7 +477,7 @@
         rows = slice(which * half, which * half + half)
         for sp in range(2):
             delta.append(jnp.concatenate([zeros, pr[1, sp, rows, :], d[sp], pr[0, sp, rows, :], zeros], 0))
-    p = refine(delta, emat)
+    p = refine(delta, emat, scr)
     for sp in range(2):
         st1[sp] = ca[sp] + p[sp]
         u = cb[sp] + p[2 + sp]
@@ -471,26 +485,26 @@
         outbuf[SPAN - 1, sp] = u[mid]
     done(SPAN - 1).start()
 
-    def final(at):
-        def step(a, b, i):
-            def emit(blk, sp, value):
-                b[sp, blk * 8 : blk * 8 + 8, :] = value
-                if 1 <= blk < blocks - 1:
-                    outbuf[i, sp, blk * 8 - H : blk * 8 - H + 8, :] = value
-
-            phi(a, cf, q0, 0, blocks, blocks, emit)
-            done(i).start()
-
-        @pl.loop(0, 3)
-        def _(k):
-            step(st1, st0, at + 2 * k)
-            step(st0, st1, at + 1 + 2 * k)
-
-        step(st1, st0, at + 6)
-
-    final(0)
-    st1[...] = gb[...]
-    final(SPAN)
+    def step(sources, targets, i):
+        def emits(dst, at):
+            def emit(sp, rows, cols, value):
+                dst[sp, rows, cols] = value
+                if H <= rows.start < N + H:
+                    outbuf[at, sp, shift(rows, -H), cols] = value
+
+            return emit
+
+        at = (i, SPAN + i)
+        phi([(sources[j], emits(targets[j], at[j])) for j in range(2)], cf, q0, 0, blocks, blocks)
+        for j in range(2):
+            done(at[j]).start()
+
+    @pl.loop(0, 3)
+    def _(k):
+        step((st1, gb), (st0, ga), 2 * k)
+        step((st0, ga), (st1, gb), 2 * k + 1)
+
+    step((st1, gb), (st0, ga), SPAN - 2)
     for i in range(2 * SPAN):
         done(i).wait()
     for cond, made in sends:
@@ -516,7 +530,7 @@
         V(2, W, C), V(2, W, C), V(2 * SPAN, 2, N, C),
         V(2, W1, C1), V(2, W1, C1), V(2, N // 2, C1), V(SPAN, 2, W1, C1), V(2, W1, C1),
         V(SPAN + 1, 2, W1, C1), V(2, 2, H, C1), V(2, 2, H, C1), V(2, W2, C2), V(2, W2, C2),
-        V(2, W2, C2), V(2, W2, C2), V(C, C1), V(C1, C),
+        V(2, W2, C2), V(2, W2, C2), pltpu.VMEM((C, C1), BF16), pltpu.VMEM((C1, C), BF16), V(C1 // L, 8 * W1, L),
         D(7), D(2, 4), D(2), D(3), D(2), D(3), D(2), D(3), D(SPAN, 3), D(SPAN), D(3), D(2),
         D(2 * SPAN), D(96),
     ]
@@ -527,13 +541,13 @@
     return pl.pallas_call(
         body,
         out_shape=jax.ShapeDtypeStruct(guess.shape, F32),
-        in_specs=[pl.BlockSpec(memory_space=pl.ANY)] * 6,
+        in_specs=[pl.BlockSpec(memory_space=pltpu.HBM)] * 6,
         out_specs=pl.BlockSpec(memory_space=pl.ANY),
         scratch_shapes=scratch,
         compiler_params=pltpu.CompilerParams(
-            collective_id=0, has_side_effects=True, vmem_limit_bytes=64 * 1024 * 1024
+            collective_id=0, has_side_effects=True, vmem_limit_bytes=48 * 1024 * 1024
         ),
-    )(initial, guess, kappa, feed, kill, react)
+    )(*[pltpu.with_memory_space_constraint(x, pltpu.HBM) for x in (initial, guess, kappa, feed, kill, react)])
 
 
 def solution(mesh):

time: 44.3 us -> 43.6 us (0.984)
  local copies, waits for them, and re-layouts: 3.19 us -> 1.32 us
  Pallas kernels: 41 us -> 42.2 us
    unnamed x1, local copies, waits for them, and re-layouts: 3.19 us -> 1.32 us
    pallas_call x1, Pallas kernels: 41 us -> 42.2 us  [local(): pl.pallas_call(body, out_shape=jax.ShapeDtypeStruct(guess.shape, F32), in...]
where the time goes in v3:
time: 43.6 us; the launch traced here: 43.5 us
  Pallas kernels  42.2 us (97%)
  local copies, waits for them, and re-layouts  1.32 us (3%)
    pallas_call x1, Pallas kernels, local(): pl.pallas_call(body, out_shape=jax.ShapeDtypeStruct(guess.shape, F32), in...  42.2 us
    unnamed x1, local copies, waits for them, and re-layouts  1.32 us

profile of v3, /device:TPU:20, one launch (start us, length us, event | category | flops | bytes accessed | tf_op | source)
XLA Modules:
  0.0 43.5 jit_solution(6397652715219743867)
XLA Ops:
  0.0 42.2 %shard_map.64 = f32[16,2,32,512]{3,2,1,0:T(8,128)S(1)} custom-call(f32[2,32,512]{2,1,0:T(8,128)} %refs_0_.1, f32[16,2,32,512]{3,2,1,0:T(8,128)} %refs_1_.1, f32[2,32,512]{2,1,0:T(8,128)} %refs_2_.1, f32[32,512]{1,0:T(8,128)} %refs_3_.1, f32[32,512]{1,0:T(8,128)} %refs_4_.1, f32[32,512]{1,0:T(8,128)} %refs_5_.1), custom_call_target="tpu_custom_call" | custom-call | tf_op jit(solution)/shard_map/pallas_call | solution.py:541
  42.2 1.3 %copy.8 = f32[16,2,32,512]{3,2,1,0:T(8,128)} copy(f32[16,2,32,512]{3,2,1,0:T(8,128)S(1)} %shard_map.64) | data formatting | bytes 4194304

commit v4 on v3

--- a/solution.py
+++ b/solution.py
@@ -14,19 +14,17 @@
 L = 128
 
 
-def phi(jobs, coef, quad, first, last, total):
-    tiles = jobs[0][0].shape[-1] // L
+def phi(jobs, coef, quad, first, last):
+    tiles = jobs[0][0].shape[1]
     lane = lax.broadcasted_iota(jnp.int32, (8, L), 1)
-    row = lax.broadcasted_iota(jnp.int32, (8, L), 0)
     low, high = lane == 0, lane == L - 1
-    top, bottom = row == 0, row == 7
     cache = {}
 
     def load(job, b, sp, c):
         key = (job, b, sp, c)
         if key not in cache:
-            x = jobs[job][0][sp, b * 8 : b * 8 + 8, c * L : c * L + L]
-            cache[key] = (x, pltpu.roll(x, 1, 0), pltpu.roll(x, 7, 0), pltpu.roll(x, 1, 1), pltpu.roll(x, L - 1, 1))
+            x = jobs[job][0][sp, c, H + b * 8 : H + b * 8 + 8, :]
+            cache[key] = (x, pltpu.roll(x, 1, 1), pltpu.roll(x, L - 1, 1))
         return cache[key]
 
     for blk in range(first, last):
@@ -38,13 +36,12 @@
             for job, (_, emit) in enumerate(jobs):
                 x, around = [], []
                 for sp in range(2):
-                    v, above, below, left, right = load(job, blk, sp, c)
-                    if blk > 0:
-                        above = jnp.where(top, load(job, blk - 1, sp, c)[1], above)
-                    if blk < total - 1:
-                        below = jnp.where(bottom, load(job, blk + 1, sp, c)[2], below)
-                    left = jnp.where(low, load(job, blk, sp, c - 1)[3] if c > 0 else 0.0, left)
-                    right = jnp.where(high, load(job, blk, sp, c + 1)[4] if c < tiles - 1 else 0.0, right)
+                    v, left, right = load(job, blk, sp, c)
+                    at = H + blk * 8
+                    above = jobs[job][0][sp, c, at - 1 : at + 7, :]
+                    below = jobs[job][0][sp, c, at + 1 : at + 9, :]
+                    left = jnp.where(low, load(job, blk, sp, c - 1)[1] if c > 0 else 0.0, left)
+                    right = jnp.where(high, load(job, blk, sp, c + 1)[2] if c < tiles - 1 else 0.0, right)
                     x.append(v)
                     around.append((above + below) + (left + right))
                 r = k[3] * x[0] * (x[1] * x[1])
@@ -52,11 +49,28 @@
                 emit(1, rows, cols, q[1] * x[1] + k[1] * around[1] + r)
 
 
+def put(dst, sp, rows, cols, value):
+    dst[sp, cols.start // L, rows.start + H : rows.stop + H, :] = value
+
+
 def into(dst):
-    def emit(sp, rows, cols, value):
-        dst[sp, rows, cols] = value
-
-    return emit
+    return lambda sp, rows, cols, value: put(dst, sp, rows, cols, value)
+
+
+def tiled(dst, src):
+    for sp in range(2):
+        x = src[sp]
+        for c in range(dst.shape[1]):
+            dst[sp, c, H : H + x.shape[0], :] = x[:, c * L : c * L + L]
+
+
+def flat(src, rows):
+    rows = slice(rows.start + H, rows.stop + H)
+    tiles = src.shape[1]
+    return [
+        jnp.concatenate([src[sp, c, rows, :] for c in range(tiles)], 1) if tiles > 1 else src[sp, 0, rows, :]
+        for sp in range(2)
+    ]
 
 
 def times(x, matrix):
@@ -112,7 +126,7 @@
 def kernel(
     T, S,
     initial, guess, kappa, feed, kill, react, out,
-    cf, q0, c1, q1, c2, q2, ga, gb, ca, cb, cc, st0, st1, outbuf,
+    cf, q0, c1, q1, c2, q2, ga, gb, ca, cb, cc, st0, st1, sb0, sb1, outbuf,
     wa, wb, wc, gs, vs, vv, ps, pr, ei, eo, zz, zy, cmat, emat, scr,
     s_loc, r_cf, r_gb, r_ga, r_c1, r_ca, r_cb, r_vs, r_gs, r_fw, r_e, r_d, s_out, s_send,
 ):
@@ -250,6 +264,9 @@
     jj = lax.broadcasted_iota(jnp.int32, emat.shape, 1) - 2 * lax.broadcasted_iota(jnp.int32, emat.shape, 0)
     emat[...] = jnp.where((jj == 0) | (jj == 1), 1.0, 0.0).astype(BF16)
     eo[...] = jnp.zeros(eo.shape, F32)
+    for ref, n in ((st0, N), (st1, N), (sb0, N), (sb1, N), (vv, N1), (zz, N2), (zy, N2)):
+        for at in (0, n + 3 * H):
+            ref[..., at : at + H, :] = jnp.zeros(ref.shape[:-2] + (H, L), F32)
 
     for c in local:
         c.wait()
@@ -293,15 +310,16 @@
     blocks = (N + 2 * H) // 8
 
     def interval(src):
-        st1[...] = src[...]
+        tiled(st1, src)
 
         @pl.loop(0, SPAN // 2)
         def _(_):
-            phi([(st1, into(st0))], cf, q0, 0, blocks, blocks)
-            phi([(st0, into(st1))], cf, q0, 0, blocks, blocks)
+            phi([(st1, into(st0))], cf, q0, 0, blocks)
+            phi([(st0, into(st1))], cf, q0, 0, blocks)
 
     interval(gb)
-    cc[...] = st1[:, mid, :]
+    for sp, x in enumerate(flat(st1, mid)):
+        cc[sp] = x
     begin(further, [(cc, ca.at[:, mid], r_ca.at[1], t + 1, s)])
     for ds in (-1, 1):
         src, dst = edge(N, ds)
@@ -316,7 +334,8 @@
     for ds in (-1, 1):
         arrive(has[-ds], [(ga.at[:, edge(N, ds)[1]], r_ga.at[ds + 1])])
     interval(ga)
-    cb[:, mid, :] = st1[:, mid, :]
+    for sp, x in enumerate(flat(st1, mid)):
+        cb[sp, mid, :] = x
     for ds in (-1, 1):
         src, dst = edge(N, ds)
         begin(has[ds], [(cb.at[:, shift(src, H)], cb.at[:, dst], r_cb.at[(ds + 1) // 2], t, s + ds)])
@@ -354,7 +373,8 @@
                 g = g - last * wc[sp, own, cols]
             gs[slot, sp, rows, cols] = g
 
-        phi([(w, emit)], c1, q1, 1, blocks1 - 1, blocks1)
+        tiled(vv.at[SPAN], w)
+        phi([(vv.at[SPAN], emit)], c1, q1, 1, blocks1 - 1)
         begin(None, [
             (gs.at[slot, :, inner], gs.at[slot, :, inner], r_gs.at[slot, 1], base + to, s)
             for to in (across, partner)
@@ -367,7 +387,7 @@
             ])
 
     interval(ca)
-    forcing(0, wa, coarsen([st1[0, mid, :], st1[1, mid, :]], False, cmat, scr))
+    forcing(0, wa, coarsen(flat(st1, mid), False, cmat, scr))
     for k, x in enumerate(coarsen([cc[0], cc[1]], False, cmat, scr)):
         wc[k] = x
     for ds in (-1, 1):
@@ -375,7 +395,7 @@
     for k, x in enumerate(coarsen([cb[0], cb[1]], True, cmat, scr)):
         wb[k] = x
     interval(cb)
-    forcing(1, wb, coarsen([st1[0, mid, :], st1[1, mid, :]], False, cmat, scr))
+    forcing(1, wb, coarsen(flat(st1, mid), False, cmat, scr))
 
     for which in range(2):
         slot = 2 * across + which
@@ -387,9 +407,9 @@
     arrive(jnp.logical_not(first), [(vs.at[:, inner], r_vs.at[1])])
     for ds in (-1, 1):
         arrive(has[-ds], [(vs.at[:, edge(N1, ds)[1]], r_vs.at[ds + 1])])
-    vv[0] = vs[...]
+    tiled(vv.at[0], vs)
     for sp, x in enumerate(coarsen([vs[0], vs[1]], True, cmat, scr)):
-        zz[sp] = x
+        zz[sp, 0, H : H + x.shape[0], :] = x
     top = (N2 + 2 * H) // 8
 
     def emit_old(sp, rows, cols, value):
@@ -398,7 +418,7 @@
     def emit_new(sp, rows, cols, value):
         eo[sp, rows, cols] = eo[sp, rows, cols] + value
 
-    phi([(zz, emit_old)], c2, q2, 1, top - 1, top)
+    phi([(zz, emit_old)], c2, q2, 1, top - 1)
 
     for which in range(2):
         slot = 2 * partner + which
@@ -417,19 +437,19 @@
         @pl.loop(0, count)
         def _(i):
             def emit(sp, rows, cols, value):
-                vv[i + 1, sp, rows, cols] = value + gs[i, sp, rows, cols]
-
-            phi([(vv.at[i], emit)], c1, q1, 0, blocks1, blocks1)
+                put(vv.at[i + 1], sp, rows, cols, value + gs[i, sp, rows, cols])
+
+            phi([(vv.at[i], emit)], c1, q1, 0, blocks1)
 
     sweep(SPAN)
 
-    r = coarsen([vv[SPAN, sp, inner, :] for sp in range(2)], False, cmat, scr)
+    r = coarsen(flat(vv.at[SPAN], inner), False, cmat, scr)
     arrive(follows, [(ei.at[:, core], r_e.at[1])])
     for ds in (-1, 1):
         arrive(follows & has[-ds], [(ei.at[:, edge(N2, ds)[1]], r_e.at[ds + 1])])
     for sp in range(2):
-        zy[sp] = zz[sp] + ei[sp]
-    phi([(zy, emit_new)], c2, q2, 1, top - 1, top)
+        zy[sp, 0, H : H + ei.shape[1], :] = zz[sp, 0, H : H + ei.shape[1], :] + ei[sp]
+    phi([(zy, emit_new)], c2, q2, 1, top - 1)
     for sp in range(2):
         eo[sp, core, :] = eo[sp, core, :] + r[sp]
     begin(leads, [(eo.at[:, core], ei.at[:, core], r_e.at[1], t + GROUP, s)])
@@ -441,14 +461,15 @@
 
     p = refine([ei[0], ei[1]], emat, scr)
     for sp in range(2):
-        vv[0, sp] = vs[sp] + p[sp]
+        p[sp] = vs[sp] + p[sp]
+    tiled(vv.at[0], p)
     sweep(SPAN - 1)
-    da = vv[2 * m, :, inner, :] - wa[:, inner, :]
-    db = vv[2 * m + 1, :, inner, :] - wb[:, inner, :]
+    da = [x - wa[sp, inner, :] for sp, x in enumerate(flat(vv.at[2 * m], inner))]
+    db = [x - wb[sp, inner, :] for sp, x in enumerate(flat(vv.at[2 * m + 1], inner))]
     half = H // 2
     for sp in range(2):
-        ps[0, sp] = jnp.concatenate([da[sp, 0:half], db[sp, 0:half]], 0)
-        ps[1, sp] = jnp.concatenate([da[sp, N1 - half :], db[sp, N1 - half :]], 0)
+        ps[0, sp] = jnp.concatenate([da[sp][0:half], db[sp][0:half]], 0)
+        ps[1, sp] = jnp.concatenate([da[sp][N1 - half :], db[sp][N1 - half :]], 0)
     for ds in (-1, 1):
         k = (ds + 1) // 2
         begin(has[ds], [(ps.at[k], pr.at[k], r_d.at[k], t, s + ds)])
@@ -458,11 +479,12 @@
 
     p = refine([eo[0], eo[1]], emat, scr)
     for sp in range(2):
-        vv[SPAN, sp, inner, :] = wc[sp] + p[sp][inner]
+        x = wc[sp] + p[sp][inner]
+        for c in range(vv.shape[2]):
+            vv[SPAN, sp, c, 2 * H : 2 * H + N1, :] = x[:, c * L : c * L + L]
     zeros = jnp.zeros((H, c1.shape[2]), F32)
-    tail = [
-        jnp.concatenate([zeros, vv[2 * m + 2, sp, inner, :] - wc[sp], zeros], 0) for sp in range(2)
-    ]
+    last = flat(vv.at[2 * m + 2], inner)
+    tail = [jnp.concatenate([zeros, last[sp] - wc[sp], zeros], 0) for sp in range(2)]
     p = refine(tail, emat, scr)
     for sp in range(2):
         outbuf[2 * SPAN - 1, sp] = cc[sp] + p[sp][mid]
@@ -479,32 +501,33 @@
             delta.append(jnp.concatenate([zeros, pr[1, sp, rows, :], d[sp], pr[0, sp, rows, :], zeros], 0))
     p = refine(delta, emat, scr)
     for sp in range(2):
-        st1[sp] = ca[sp] + p[sp]
         u = cb[sp] + p[2 + sp]
-        gb[sp] = u
+        for c in range(st1.shape[1]):
+            st1[sp, c, H : H + u.shape[0], :] = ca[sp, :, c * L : c * L + L] + p[sp][:, c * L : c * L + L]
+            sb1[sp, c, H : H + u.shape[0], :] = u[:, c * L : c * L + L]
         outbuf[SPAN - 1, sp] = u[mid]
     done(SPAN - 1).start()
 
     def step(sources, targets, i):
         def emits(dst, at):
             def emit(sp, rows, cols, value):
-                dst[sp, rows, cols] = value
+                put(dst, sp, rows, cols, value)
                 if H <= rows.start < N + H:
                     outbuf[at, sp, shift(rows, -H), cols] = value
 
             return emit
 
         at = (i, SPAN + i)
-        phi([(sources[j], emits(targets[j], at[j])) for j in range(2)], cf, q0, 0, blocks, blocks)
+        phi([(sources[j], emits(targets[j], at[j])) for j in range(2)], cf, q0, 0, blocks)
         for j in range(2):
             done(at[j]).start()
 
     @pl.loop(0, 3)
     def _(k):
-        step((st1, gb), (st0, ga), 2 * k)
-        step((st0, ga), (st1, gb), 2 * k + 1)
-
-    step((st1, gb), (st0, ga), SPAN - 2)
+        step((st1, sb1), (st0, sb0), 2 * k)
+        step((st0, sb0), (st1, sb1), 2 * k + 1)
+
+    step((st1, sb1), (st0, sb0), SPAN - 2)
     for i in range(2 * SPAN):
         done(i).wait()
     for cond, made in sends:
@@ -527,10 +550,10 @@
     scratch = [
         V(5, W, C), V(2, W, C), V(5, W1, C1), V(2, W1, C1), V(5, W2, C2), V(2, W2, C2),
         V(2, W, C), V(2, W, C), V(2, W, C), V(2, W, C), V(2, N, C),
-        V(2, W, C), V(2, W, C), V(2 * SPAN, 2, N, C),
+        *[V(2, C // L, W + 2 * H, L) for _ in range(4)], V(2 * SPAN, 2, N, C),
         V(2, W1, C1), V(2, W1, C1), V(2, N // 2, C1), V(SPAN, 2, W1, C1), V(2, W1, C1),
-        V(SPAN + 1, 2, W1, C1), V(2, 2, H, C1), V(2, 2, H, C1), V(2, W2, C2), V(2, W2, C2),
-        V(2, W2, C2), V(2, W2, C2), pltpu.VMEM((C, C1), BF16), pltpu.VMEM((C1, C), BF16), V(C1 // L, 8 * W1, L),
+        V(SPAN + 1, 2, C1 // L, W1 + 2 * H, L), V(2, 2, H, C1), V(2, 2, H, C1), V(2, W2, C2), V(2, W2, C2),
+        V(2, C2 // L, W2 + 2 * H, L), V(2, C2 // L, W2 + 2 * H, L), pltpu.VMEM((C, C1), BF16), pltpu.VMEM((C1, C), BF16), V(C1 // L, 8 * W1, L),
         D(7), D(2, 4), D(2), D(3), D(2), D(3), D(2), D(3), D(SPAN, 3), D(SPAN), D(3), D(2),
         D(2 * SPAN), D(96),
     ]

time: 43.6 us -> 43.6 us (level)
  no operation moved by 1% of the time
where the time goes in v4:
time: 43.6 us; the launch traced here: 43.5 us
  Pallas kernels  42.1 us (97%)
  local copies, waits for them, and re-layouts  1.32 us (3%)
    pallas_call x1, Pallas kernels, local(): pl.pallas_call(body, out_shape=jax.ShapeDtypeStruct(guess.shape, F32), in...  42.1 us
    unnamed x1, local copies, waits for them, and re-layouts  1.32 us

profile of v4, /device:TPU:20, one launch (start us, length us, event | category | flops | bytes accessed | tf_op | source)
XLA Modules:
  0.0 43.5 jit_solution(2620645957785441434)
XLA Ops:
  0.0 42.1 %shard_map.64 = f32[16,2,32,512]{3,2,1,0:T(8,128)S(1)} custom-call(f32[2,32,512]{2,1,0:T(8,128)} %refs_0_.1, f32[16,2,32,512]{3,2,1,0:T(8,128)} %refs_1_.1, f32[2,32,512]{2,1,0:T(8,128)} %refs_2_.1, f32[32,512]{1,0:T(8,128)} %refs_3_.1, f32[32,512]{1,0:T(8,128)} %refs_4_.1, f32[32,512]{1,0:T(8,128)} %refs_5_.1), custom_call_target="tpu_custom_call" | custom-call | tf_op jit(solution)/shard_map/pallas_call | solution.py:564
  42.1 1.3 %copy.8 = f32[16,2,32,512]{3,2,1,0:T(8,128)} copy(f32[16,2,32,512]{3,2,1,0:T(8,128)S(1)} %shard_map.64) | data formatting | bytes 4194304

commit v5 on v4

--- a/solution.py
+++ b/solution.py
@@ -290,7 +290,6 @@
         ])
     for ds in (-1, 1):
         src, dst = edge(N, ds)
-        src1, dst1 = edge(N1, ds)
         begin(further & has[ds], [
             (guess.at[2 * SPAN - 1, :, src], ga.at[:, dst], r_ga.at[ds + 1], t + 1, s + ds),
         ])
@@ -298,9 +297,6 @@
             (initial.at[:, src], ga.at[:, dst], r_ga.at[ds + 1], t, s + ds),
             (initial.at[:, src], ca.at[:, dst], r_ca.at[ds + 1], t, s + ds),
         ])
-        begin(has[ds], [
-            (c1.at[:, shift(src1, H)], c1.at[:, dst1], r_c1.at[(ds + 1) // 2], t, s + ds),
-        ])
 
     def quads(coef, quad):
         quad[0] = 1.0 - coef[2] - 4.0 * coef[0]
@@ -342,11 +338,8 @@
 
     arrive(jnp.logical_not(opening), [(ca.at[:, mid], r_ca.at[1])])
     for ds in (-1, 1):
-        arrive(has[-ds], [
-            (ca.at[:, edge(N, ds)[1]], r_ca.at[ds + 1]),
-            (c1.at[:, edge(N1, ds)[1]], r_c1.at[(ds + 1) // 2]),
-        ])
-    quads(c1, q1)
+        arrive(has[-ds], [(ca.at[:, edge(N, ds)[1]], r_ca.at[ds + 1])])
+    quads(c1.at[:, inner], q1.at[:, inner])
     blocks1 = (N1 + 2 * H) // 8
     for k, x in enumerate(coarsen([ca[0], ca[1]], True, cmat, scr)):
         wa[k] = x
@@ -355,12 +348,9 @@
     def _():
         vs[:, inner, :] = wa[:, inner, :]
 
-    begin(first, [(wa.at[:, inner], vs.at[:, inner], r_vs.at[1], base + r, s) for r in range(1, GROUP)])
     for ds in (-1, 1):
         src, dst = edge(N1, ds)
-        begin(first & has[ds], [
-            (wa.at[:, shift(src, H)], vs.at[:, dst], r_vs.at[ds + 1], base + r, s + ds) for r in range(GROUP)
-        ])
+        begin(first & has[ds], [(wa.at[:, shift(src, H)], vs.at[:, dst], r_vs.at[ds + 1], t, s + ds)])
 
     def forcing(which, w, r):
         slot = 2 * m + which
@@ -375,16 +365,15 @@
 
         tiled(vv.at[SPAN], w)
         phi([(vv.at[SPAN], emit)], c1, q1, 1, blocks1 - 1)
-        begin(None, [
-            (gs.at[slot, :, inner], gs.at[slot, :, inner], r_gs.at[slot, 1], base + to, s)
-            for to in (across, partner)
-        ])
         for ds in (-1, 1):
             src, dst = edge(N1, ds)
-            begin(has[ds], [
-                (gs.at[slot, :, shift(src, H)], gs.at[slot, :, dst], r_gs.at[slot, ds + 1], base + to, s + ds)
-                for to in (across, partner, m)
-            ])
+            begin(has[ds], [(gs.at[slot, :, shift(src, H)], gs.at[slot, :, dst], r_gs.at[slot, ds + 1], t, s + ds)])
+
+    def spread(which):
+        slot = 2 * m + which
+        for ds in (-1, 1):
+            arrive(has[-ds], [(gs.at[slot, :, edge(N1, ds)[1]], r_gs.at[slot, ds + 1])])
+        begin(None, [(gs.at[slot], gs.at[slot], r_gs.at[slot, 1], base + to, s) for to in (across, partner)])
 
     interval(ca)
     forcing(0, wa, coarsen(flat(st1, mid), False, cmat, scr))
@@ -394,19 +383,26 @@
         arrive(has[-ds], [(cb.at[:, edge(N, ds)[1]], r_cb.at[(ds + 1) // 2])])
     for k, x in enumerate(coarsen([cb[0], cb[1]], True, cmat, scr)):
         wb[k] = x
+    spread(0)
+    for ds in (-1, 1):
+        arrive(first & has[-ds], [(vs.at[:, edge(N1, ds)[1]], r_vs.at[ds + 1])])
+    begin(first, [(vs, vs, r_vs.at[1], base + r, s) for r in range(1, GROUP)])
+    for ds in (-1, 1):
+        src, dst = edge(N1, ds)
+        begin(has[ds], [
+            (c1.at[:, shift(src, H)], c1.at[:, dst], r_c1.at[(ds + 1) // 2], t, s + ds),
+        ])
     interval(cb)
     forcing(1, wb, coarsen(flat(st1, mid), False, cmat, scr))
 
+    spread(1)
+
     for which in range(2):
         slot = 2 * across + which
-        arrive(None, [(gs.at[slot, :, inner], r_gs.at[slot, 1])])
-        for ds in (-1, 1):
-            arrive(has[-ds], [(gs.at[slot, :, edge(N1, ds)[1]], r_gs.at[slot, ds + 1])])
+        arrive(None, [(gs.at[slot], r_gs.at[slot, 1])])
         begin(None, [(gs.at[slot], gs.at[slot], r_fw.at[slot], base + partner, s)])
 
-    arrive(jnp.logical_not(first), [(vs.at[:, inner], r_vs.at[1])])
-    for ds in (-1, 1):
-        arrive(has[-ds], [(vs.at[:, edge(N1, ds)[1]], r_vs.at[ds + 1])])
+    arrive(jnp.logical_not(first), [(vs, r_vs.at[1])])
     tiled(vv.at[0], vs)
     for sp, x in enumerate(coarsen([vs[0], vs[1]], True, cmat, scr)):
         zz[sp, 0, H : H + x.shape[0], :] = x
@@ -420,14 +416,12 @@
 
     phi([(zz, emit_old)], c2, q2, 1, top - 1)
 
+    for ds in (-1, 1):
+        arrive(has[-ds], [(c1.at[:, edge(N1, ds)[1]], r_c1.at[(ds + 1) // 2])])
+    quads(c1, q1)
     for which in range(2):
         slot = 2 * partner + which
-        arrive(None, [(gs.at[slot, :, inner], r_gs.at[slot, 1])])
-        for ds in (-1, 1):
-            arrive(has[-ds], [
-                (gs.at[slot, :, edge(N1, ds)[1]], r_gs.at[slot, ds + 1]),
-                (gs.at[2 * m + which, :, edge(N1, ds)[1]], r_gs.at[2 * m + which, ds + 1]),
-            ])
+        arrive(None, [(gs.at[slot], r_gs.at[slot, 1])])
     other = lax.rem(partner + 2, GROUP)
     for which in range(2):
         slot = 2 * other + which

time: 43.6 us -> 45.5 us (1.044)
  the two profiles are of different devices: /device:TPU:20 before, /device:TPU:18 now
where the time goes in v5:
time: 45.5 us; the launch traced here: 45.3 us
  Pallas kernels  44 us (97%)
  local copies, waits for them, and re-layouts  1.32 us (3%)
    pallas_call x1, Pallas kernels, local(): pl.pallas_call(body, out_shape=jax.ShapeDtypeStruct(guess.shape, F32), in...  44 us
    unnamed x1, local copies, waits for them, and re-layouts  1.32 us

profile of v5, /device:TPU:18, one launch (start us, length us, event | category | flops | bytes accessed | tf_op | source)
XLA Modules:
  0.0 45.3 jit_solution(15585974904925813720)
XLA Ops:
  0.0 44.0 %shard_map.64 = f32[16,2,32,512]{3,2,1,0:T(8,128)S(1)} custom-call(f32[2,32,512]{2,1,0:T(8,128)} %refs_0_.1, f32[16,2,32,512]{3,2,1,0:T(8,128)} %refs_1_.1, f32[2,32,512]{2,1,0:T(8,128)} %refs_2_.1, f32[32,512]{1,0:T(8,128)} %refs_3_.1, f32[32,512]{1,0:T(8,128)} %refs_4_.1, f32[32,512]{1,0:T(8,128)} %refs_5_.1), custom_call_target="tpu_custom_call" | custom-call | tf_op jit(solution)/shard_map/pallas_call | solution.py:558
  44.0 1.3 %copy.8 = f32[16,2,32,512]{3,2,1,0:T(8,128)} copy(f32[16,2,32,512]{3,2,1,0:T(8,128)S(1)} %shard_map.64) | data formatting | bytes 4194304

commit v6 on v4

--- a/solution.py
+++ b/solution.py
@@ -128,7 +128,7 @@
     initial, guess, kappa, feed, kill, react, out,
     cf, q0, c1, q1, c2, q2, ga, gb, ca, cb, cc, st0, st1, sb0, sb1, outbuf,
     wa, wb, wc, gs, vs, vv, ps, pr, ei, eo, zz, zy, cmat, emat, scr,
-    s_loc, r_cf, r_gb, r_ga, r_c1, r_ca, r_cb, r_vs, r_gs, r_fw, r_e, r_d, s_out, s_send,
+    s_loc, r_cf, r_gb, r_ga, r_c1, r_ca, r_cb, r_vs, r_gs, r_e, r_d, s_out, s_send,
 ):
     t = lax.axis_index("tm")
     s = lax.axis_index("space")
@@ -145,6 +145,7 @@
     leads = t + GROUP < T
     partner = m + 1 - 2 * lax.rem(m, 2)
     across = lax.rem(m + 2, GROUP)
+    distant = lax.rem(partner + 2, GROUP)
     sends = []
     number = [0]
 
@@ -377,13 +378,13 @@
         phi([(vv.at[SPAN], emit)], c1, q1, 1, blocks1 - 1)
         begin(None, [
             (gs.at[slot, :, inner], gs.at[slot, :, inner], r_gs.at[slot, 1], base + to, s)
-            for to in (across, partner)
+            for to in (across, distant, partner)
         ])
         for ds in (-1, 1):
             src, dst = edge(N1, ds)
             begin(has[ds], [
                 (gs.at[slot, :, shift(src, H)], gs.at[slot, :, dst], r_gs.at[slot, ds + 1], base + to, s + ds)
-                for to in (across, partner, m)
+                for to in (across, distant, partner, m)
             ])
 
     interval(ca)
@@ -397,13 +398,6 @@
     interval(cb)
     forcing(1, wb, coarsen(flat(st1, mid), False, cmat, scr))
 
-    for which in range(2):
-        slot = 2 * across + which
-        arrive(None, [(gs.at[slot, :, inner], r_gs.at[slot, 1])])
-        for ds in (-1, 1):
-            arrive(has[-ds], [(gs.at[slot, :, edge(N1, ds)[1]], r_gs.at[slot, ds + 1])])
-        begin(None, [(gs.at[slot], gs.at[slot], r_fw.at[slot], base + partner, s)])
-
     arrive(jnp.logical_not(first), [(vs.at[:, inner], r_vs.at[1])])
     for ds in (-1, 1):
         arrive(has[-ds], [(vs.at[:, edge(N1, ds)[1]], r_vs.at[ds + 1])])
@@ -421,17 +415,12 @@
     phi([(zz, emit_old)], c2, q2, 1, top - 1)
 
     for which in range(2):
-        slot = 2 * partner + which
-        arrive(None, [(gs.at[slot, :, inner], r_gs.at[slot, 1])])
-        for ds in (-1, 1):
-            arrive(has[-ds], [
-                (gs.at[slot, :, edge(N1, ds)[1]], r_gs.at[slot, ds + 1]),
-                (gs.at[2 * m + which, :, edge(N1, ds)[1]], r_gs.at[2 * m + which, ds + 1]),
-            ])
-    other = lax.rem(partner + 2, GROUP)
-    for which in range(2):
-        slot = 2 * other + which
-        arrive(None, [(gs.at[slot], r_fw.at[slot])])
+        for other in (m, partner, across, distant):
+            slot = 2 * other + which
+            if other is not m:
+                arrive(None, [(gs.at[slot, :, inner], r_gs.at[slot, 1])])
+    for ds in (-1, 1):
+        arrive(has[-ds], [(gs.at[i, :, edge(N1, ds)[1]], r_gs.at[i, ds + 1]) for i in range(SPAN)])
 
     def sweep(count):
         @pl.loop(0, count)
@@ -554,7 +543,7 @@
         V(2, W1, C1), V(2, W1, C1), V(2, N // 2, C1), V(SPAN, 2, W1, C1), V(2, W1, C1),
         V(SPAN + 1, 2, C1 // L, W1 + 2 * H, L), V(2, 2, H, C1), V(2, 2, H, C1), V(2, W2, C2), V(2, W2, C2),
         V(2, C2 // L, W2 + 2 * H, L), V(2, C2 // L, W2 + 2 * H, L), pltpu.VMEM((C, C1), BF16), pltpu.VMEM((C1, C), BF16), V(C1 // L, 8 * W1, L),
-        D(7), D(2, 4), D(2), D(3), D(2), D(3), D(2), D(3), D(SPAN, 3), D(SPAN), D(3), D(2),
+        D(7), D(2, 4), D(2), D(3), D(2), D(3), D(2), D(3), D(SPAN, 3), D(3), D(2),
         D(2 * SPAN), D(96),
     ]
 

time: 43.6 us -> 44.7 us (1.025)
  Pallas kernels: 42.1 us -> 43.2 us
    pallas_call x1, Pallas kernels: 42.1 us -> 43.2 us  [local(): pl.pallas_call(body, out_shape=jax.ShapeDtypeStruct(guess.shape, F32), in...]
where the time goes in v6:
time: 44.7 us; the launch traced here: 44.6 us
  Pallas kernels  43.2 us (97%)
  local copies, waits for them, and re-layouts  1.32 us (3%)
    pallas_call x1, Pallas kernels, local(): pl.pallas_call(body, out_shape=jax.ShapeDtypeStruct(guess.shape, F32), in...  43.2 us
    unnamed x1, local copies, waits for them, and re-layouts  1.32 us

profile of v6, /device:TPU:20, one launch (start us, length us, event | category | flops | bytes accessed | tf_op | source)
XLA Modules:
  0.0 44.6 jit_solution(16144714239830411412)
XLA Ops:
  0.0 43.2 %shard_map.64 = f32[16,2,32,512]{3,2,1,0:T(8,128)S(1)} custom-call(f32[2,32,512]{2,1,0:T(8,128)} %refs_0_.1, f32[16,2,32,512]{3,2,1,0:T(8,128)} %refs_1_.1, f32[2,32,512]{2,1,0:T(8,128)} %refs_2_.1, f32[32,512]{1,0:T(8,128)} %refs_3_.1, f32[32,512]{1,0:T(8,128)} %refs_4_.1, f32[32,512]{1,0:T(8,128)} %refs_5_.1), custom_call_target="tpu_custom_call" | custom-call | tf_op jit(solution)/shard_map/pallas_call | solution.py:553
  43.2 1.3 %copy.8 = f32[16,2,32,512]{3,2,1,0:T(8,128)} copy(f32[16,2,32,512]{3,2,1,0:T(8,128)S(1)} %shard_map.64) | data formatting | bytes 4194304
